TPU v7x, 32 devices: a whole 2x2x4 slice. The times are simulated.
32 devices in a mesh: fsdp: 8 (over z, y), mem: 4 (over x, core).
Axes of the slice: x: 2, y: 2, z: 4, core: 2. Of those that a mesh axis runs over, the one named last changes fastest.
Arguments:
- suffix: bfloat16 [256, 32, 768], P('fsdp'), may hold values from -6 to 6
- memory: bfloat16 [256, 256, 768], P('fsdp', 'mem'), may hold values from -6 to 6
- counts: int32 [256], P('fsdp'), may hold values from 0 to 256, as said below
- cotangent: bfloat16 [256, 32, 768], P('fsdp'), may hold values from -6 to 6
- self_norm_gain: bfloat16 [768], P('fsdp'), may hold values from 0.5 to 1.5
- self_norm_bias: bfloat16 [768], P('fsdp'), may hold values from -1.5 to 1.5
- self_query: bfloat16 [768, 768], P('fsdp'), may hold values from -0.21875 to 0.21875
- self_key: bfloat16 [768, 768], P('fsdp'), may hold values from -0.21875 to 0.21875
- self_value: bfloat16 [768, 768], P('fsdp'), may hold values from -0.21875 to 0.21875
- self_output: bfloat16 [768, 768], P('fsdp'), may hold values from -0.4375 to 0.4375
- cross_norm_gain: bfloat16 [768], P('fsdp'), may hold values from 0.5 to 1.5
- cross_norm_bias: bfloat16 [768], P('fsdp'), may hold values from -1.5 to 1.5
- cross_query: bfloat16 [768, 768], P('fsdp'), may hold values from -0.21875 to 0.21875
- cross_key: bfloat16 [768, 768], P('fsdp'), may hold values from -0.21875 to 0.21875
- cross_value: bfloat16 [768, 768], P('fsdp'), may hold values from -0.21875 to 0.21875
- cross_output: bfloat16 [768, 768], P('fsdp'), may hold values from -1.25 to 1.25
- dense_norm_gain: bfloat16 [768], P('fsdp'), may hold values from 0.5 to 1.5
- dense_norm_bias: bfloat16 [768], P('fsdp'), may hold values from -1.5 to 1.5
- dense_in: bfloat16 [768, 3072], P('fsdp'), may hold values from -0.21875 to 0.21875
- dense_in_bias: bfloat16 [3072], P('fsdp'), may hold values from -2.5 to 2.5
- dense_out: bfloat16 [3072, 768], P('fsdp'), may hold values from -0.109375 to 0.109375
- dense_out_bias: bfloat16 [768], P('fsdp'), may hold values from -2.5 to 2.5
Outputs:
- block_output: bfloat16 [256, 32, 768], P('fsdp')
- suffix_grad: bfloat16 [256, 32, 768], P('fsdp')
- memory_grad: bfloat16 [256, 256, 768], P('fsdp', 'mem')
- self_norm_gain_grad: float32 [768], P('fsdp')
- self_norm_bias_grad: float32 [768], P('fsdp')
- self_query_grad: float32 [768, 768], P('fsdp')
- self_key_grad: float32 [768, 768], P('fsdp')
- self_value_grad: float32 [768, 768], P('fsdp')
- self_output_grad: float32 [768, 768], P('fsdp')
- cross_norm_gain_grad: float32 [768], P('fsdp')
- cross_norm_bias_grad: float32 [768], P('fsdp')
- cross_query_grad: float32 [768, 768], P('fsdp')
- cross_key_grad: float32 [768, 768], P('fsdp')
- cross_value_grad: float32 [768, 768], P('fsdp')
- cross_output_grad: float32 [768, 768], P('fsdp')
- dense_norm_gain_grad: float32 [768], P('fsdp')
- dense_norm_bias_grad: float32 [768], P('fsdp')
- dense_in_grad: float32 [768, 3072], P('fsdp')
- dense_in_bias_grad: float32 [3072], P('fsdp')
- dense_out_grad: float32 [3072, 768], P('fsdp')
- dense_out_bias_grad: float32 [768], P('fsdp')
Inputs may be any that keep to these rules, and one draw needn't show every extreme that they name: memory slots that an example may read are its first counts ones; in every aligned group of 32 examples one example has 256 and another has none.
All inputs are finite; a program needn't handle non-finite values.
Results may differ from a plain program's by a relative error of at most 0.019.
Values may be sent and summed in bfloat16 or wider, within the bound.
No kernel may reach another device: no remote copies, remote signals or barrier semaphores. Data moves between devices by JAX's collectives and lax.ppermute only.
A program may use at most 256 MiB of HBM per device.

v0:
```python
import functools

import jax
import jax.numpy as jnp
from jax import lax
from jax.experimental import pallas as pl
from jax.experimental.pallas import tpu as pltpu
from jax.sharding import PartitionSpec as P

HEADS = 12
HEAD = 64
TOGETHER = 4
GROUPS = HEADS // TOGETHER
LANES = TOGETHER * HEAD
SCALE = HEAD ** (-0.5)
BF = jnp.bfloat16
F32 = jnp.float32
ANY = pl.BlockSpec(memory_space=pl.ANY)
SMEM = pl.BlockSpec(memory_space=pltpu.SMEM)
VMEM = pl.BlockSpec(memory_space=pltpu.VMEM)


def swap(value, axis, distance):
    size = lax.axis_size(axis)
    return lax.ppermute(value, axis, [(i, i ^ distance) for i in range(size)])


def after(value, *others):
    return lax.optimization_barrier((value, *others))[0] if others else value


def fsdp_split(size):
    slow = 4 if size % 4 == 0 else 1
    return slow, size // slow


def dot(left, right):
    return jnp.dot(left, right, preferred_element_type=F32)


def dot_nt(left, right):
    return lax.dot_general(left, right, (((1,), (1,)), ((), ())), preferred_element_type=F32)


def dot_tn(left, right):
    return lax.dot_general(left, right, (((0,), (0,)), ((), ())), preferred_element_type=F32)


def rows_of(start, size):
    return pl.ds(pl.multiple_of(start, 16), size)


def block(ref, by_rows, shard, which):
    if by_rows:
        return ref.at[shard, pl.ds(which * 2, 2)]
    rows = ref.shape[1] // SHARDS[0]
    return ref.at[pl.ds(which * 2, 2), rows_of(shard * rows, rows)]


SHARDS = [0]


class Copies:
    def __init__(self, sems):
        self.sems = sems
        self.next = 0

    def start(self, source, target):
        copy = pltpu.make_async_copy(source, target, self.sems.at[self.next])
        self.next += 1
        copy.start()
        return copy


def wait_all(copies):
    for copy in copies:
        copy.wait()


def load_weight(where, whole, weights, copies, by_rows=False):
    z, y, c = where[0], where[1], where[2]
    rows = whole.shape[2] if by_rows else whole.shape[1] // SHARDS[0]
    started = []
    for which, pieces in ((c, weights[0]), (1 - c, weights[1])):
        fast = len(pieces)
        for b, piece in enumerate(pieces):
            for k in range(piece.shape[0]):
                shard = (z ^ k) * fast + (y ^ b)
                for i in range(2):
                    source = piece.at[k, pl.ds(i * rows, rows)]
                    if by_rows:
                        target = whole.at[shard, 2 * which + i]
                    else:
                        target = whole.at[2 * which + i, rows_of(shard * rows, rows)]
                    started.append(copies.start(source, target))
    return started


def store_grad(where, whole, near, far, theirs, copies, by_rows=False):
    y, c = where[1], where[2]
    slow, cut = near.shape[0], near.shape[0] // 2
    fast = (len(theirs) + 1) // 2
    started = []
    for b in range(fast):
        for k in range(slow):
            shard = k * fast + (y ^ b)
            mine = far.at[b - 1, k] if b else near.at[k]
            other = theirs[2 * b - 1 + k // cut].at[k % cut] if b else theirs[0].at[k]
            started.append(copies.start(block(whole, by_rows, shard, 1 - c), other))
            started.append(copies.start(block(whole, by_rows, shard, c), mine))
    return started


def my_examples(where, source, target, copies):
    count = target.shape[0]
    return copies.start(source.at[pl.ds(where[3] * count, count)], target)


def normalise(values):
    centred = values - jnp.mean(values, axis=-1, keepdims=True)
    scale = lax.rsqrt(jnp.mean(centred * centred, axis=-1, keepdims=True) + 1e-06)
    return centred * scale, scale


def norm_back(grad, gain, hat, scale):
    inner = grad * gain
    mean = jnp.mean(inner, axis=-1, keepdims=True)
    along = jnp.mean(inner * hat, axis=-1, keepdims=True)
    return (
        scale * (inner - mean - hat * along),
        jnp.sum(grad * hat, axis=0, keepdims=True),
        jnp.sum(grad, axis=0, keepdims=True),
    )


def head_mask(rows):
    shape = (TOGETHER * rows, LANES)
    row = lax.broadcasted_iota(jnp.int32, shape, 0) // rows
    lane = lax.broadcasted_iota(jnp.int32, shape, 1) // HEAD
    return (row == lane).astype(F32)


def stack_heads(value, mask):
    return (jnp.concatenate([value] * TOGETHER, axis=0).astype(F32) * mask).astype(BF)


def merge_heads(value, mask):
    rows = value.shape[0] // TOGETHER
    value = value * mask
    total = value[:rows]
    for h in range(1, TOGETHER):
        total = total + value[h * rows : (h + 1) * rows]
    return total


def columns(j, width):
    return slice(j * width, (j + 1) * width)


def self_forward(
    group, where, suffix, weights, x1, a1, qkv, p1, o1, vec, weight, start, small, sems
):
    rows, width = x1.shape
    copies = Copies(sems)
    first = my_examples(where, suffix, start, copies)
    fast, slow = len(weights[0]), weights[0][0].shape[0]
    part = width // (fast * slow)
    vectors = []
    for b, piece in enumerate(weights[0]):
        for k in range(slow):
            source = piece.at[k, pl.ds(2 * part, 16), pl.ds(0, 128)]
            vectors.append(copies.start(source, small.at[b * slow + k]))
    loads = load_weight(where, weight, weights, copies)
    wait_all(vectors)
    lane = lax.broadcasted_iota(jnp.int32, (128, width), 0)
    place = lax.broadcasted_iota(jnp.int32, (128, width), 1) - lane
    together = jnp.zeros(vec.shape, F32)
    for i in range(fast * slow):
        shard = (where[0] ^ (i % slow)) * fast + (where[1] ^ (i // slow))
        chosen = ((place == shard * part) & (lane < part)).astype(F32).astype(BF)
        together = together + dot(small[i], chosen)
    vec[...] = together
    first.wait()
    values = start[...].reshape(rows, width).astype(F32)
    hat, _ = normalise(values)
    a1[...] = (hat * vec[0:1, :] + vec[1:2, :]).astype(BF)
    wait_all(loads)
    for j in range(3):
        qkv[:, columns(j, width)] = dot(a1[...], weight[j]).astype(BF)
    mask = head_mask(group)
    length = suffix.shape[1]
    shape = (TOGETHER * group, group)
    row = lax.broadcasted_iota(jnp.int32, shape, 0) % group
    col = lax.broadcasted_iota(jnp.int32, shape, 1)
    seen = (row // length == col // length) & (row >= col)
    for r in range(rows // group):
        here = columns(r, group)
        for g in range(GROUPS):
            lanes = [slice(i * width + g * LANES, i * width + (g + 1) * LANES) for i in range(3)]
            queries = stack_heads(qkv[here, lanes[0]], mask)
            scores = dot_nt(queries, qkv[here, lanes[1]]) * SCALE
            scores = jnp.where(seen, scores, -1e30)
            powers = jnp.exp(scores - jnp.max(scores, axis=-1, keepdims=True))
            probs = (powers / jnp.sum(powers, axis=-1, keepdims=True)).astype(BF)
            p1[r * GROUPS + g] = probs
            found = dot(probs, qkv[here, lanes[2]])
            o1[here, lanes[0]] = merge_heads(found, mask).astype(BF)
    x1[...] = values + dot(o1[...], weight[3])


def cross_forward(
    where, counts, x1, vec, memory, weights, x2, a2, q2, kv, p2, o2, weight, sems
):
    rows, width = x1.shape
    examples = pl.num_programs(0)
    e = pl.program_id(0)
    total = kv.shape[1]
    length = p2.shape[2] // TOGETHER

    @pl.when(e == 0)
    def _():
        loads = load_weight(where, weight, weights, Copies(sems))
        hat, _ = normalise(x1[...])
        a2[...] = (hat * vec[2:3, :] + vec[3:4, :]).astype(BF)
        wait_all(loads)
        q2[...] = dot(a2[...], weight[0]).astype(BF)

    tokens = memory[...].reshape(total, width)
    for j in range(2):
        kv[0, :, columns(j, width)] = dot(tokens, weight[1 + j]).astype(BF)
    mask = head_mask(length)
    position = lax.broadcasted_iota(jnp.int32, (1, total), 1)
    valid = position < counts[where[3] * examples + e]
    here = rows_of(e * length, length)
    probs = []
    for g in range(GROUPS):
        lanes = columns(g, LANES)
        queries = stack_heads(q2[here, lanes], mask)
        scores = dot_nt(queries, kv[0, :, lanes]) * SCALE
        scores = jnp.where(valid, scores, -1e30)
        top = jnp.maximum(jnp.max(scores, axis=-1, keepdims=True), 0.0)
        powers = jnp.exp(scores - top)
        weight_sum = jnp.sum(powers, axis=-1, keepdims=True) + jnp.exp(-top)
        probs.append((powers / weight_sum).astype(BF))
    for g in range(GROUPS):
        p2[0, g] = probs[g]
        found = dot(probs[g], kv[0, :, width + g * LANES : width + (g + 1) * LANES])
        o2[here, columns(g, LANES)] = merge_heads(found, mask).astype(BF)

    @pl.when(e == examples - 1)
    def _():
        x2[...] = x1[...] + dot(o2[...], weight[3])


def dense_inner(
    where, x2, vec, bias, cotangent, weights, a3, h, slope, near, far, theirs,
    weight, grad, cot, sems,
):
    rows, width = x2.shape
    copies = Copies(sems)
    cot_copy = my_examples(where, cotangent, cot, copies)
    loads = load_weight(where, weight, weights, copies)
    hat, _ = normalise(x2[...])
    a3[...] = (hat * vec[4:5, :] + vec[5:6, :]).astype(BF)
    cot_copy.wait()
    gy = cot[...].reshape(rows, width)
    wait_all(loads)
    flat = grad.shape[0] * grad.shape[1] * grad.shape[2]
    step = flat // grad.shape[0]
    for j in range(4):
        for half in range(2):
            cols = slice(j * width + half * 384, j * width + (half + 1) * 384)
            u = dot(a3[...], weight[j, :, half * 384 : (half + 1) * 384]) + bias[:, cols]
            square = u * u
            t = jnp.tanh(0.7978845608 * u * (1.0 + 0.044715 * square))
            h[:, cols] = (0.5 * u * (1.0 + t)).astype(BF)
            slope[:, cols] = (
                0.5 * (1.0 + t)
                + (0.5 * 0.7978845608) * u * (1.0 - t * t) * (1.0 + (3.0 * 0.044715) * square)
            ).astype(BF)
            part = dot_tn(h[:, cols], gy).astype(BF)
            per = 384 // step
            grad[cols.start // step : cols.start // step + per] = part.reshape(
                (per,) + grad.shape[1:]
            )
    wait_all(store_grad(where, grad, near, far, theirs, Copies(sems), True))


def dense_outer(
    where, x2, vec, a3, h, slope, cotangent, weights, y, du, vecs, bias_grad, near, far, theirs,
    weight, grad, cot, sems,
):
    rows, width = x2.shape
    copies = Copies(sems)
    cot_copy = my_examples(where, cotangent, cot, copies)
    wait_all(load_weight(where, weight, weights, copies, True))
    cot_copy.wait()
    gy = cot[...].reshape(rows, width)
    shards = weight.shape[0]
    step = weight.shape[1] * weight.shape[2]
    whole = weight[...].reshape(shards * step, width)
    for j in range(4):
        cols = columns(j, width)
        low = (dot_nt(gy, whole[cols]) * slope[:, cols].astype(F32)).astype(BF)
        du[:, cols] = low
        bias_grad[:, cols] = jnp.sum(low.astype(F32), axis=0, keepdims=True)
        grad[j] = dot_tn(a3[...], low).astype(BF)
    started = store_grad(where, grad, near, far, theirs, Copies(sems))
    result = x2[...] + dot(h[...], whole) + vec[6:7, :]
    y[...] = result.astype(BF).reshape(y.shape)
    vecs[...] = jnp.sum(gy.astype(F32), axis=0, keepdims=True)
    wait_all(started)


def dense_back(where, x2, vec, du, cotangent, weights, gx2, vecs, weight, cot, sems):
    rows, width = x2.shape
    copies = Copies(sems)
    cot_copy = my_examples(where, cotangent, cot, copies)
    loads = load_weight(where, weight, weights, copies)
    hat, scale = normalise(x2[...])
    cot_copy.wait()
    wait_all(loads)
    da3 = dot_nt(du[:, columns(0, width)], weight[0])
    for j in range(1, 4):
        da3 = da3 + dot_nt(du[:, columns(j, width)], weight[j])
    back, gain_grad, shift_grad = norm_back(da3, vec[4:5, :], hat, scale)
    gx2[...] = cot[...].reshape(rows, width).astype(F32) + back
    vecs[0:1, :] = gain_grad
    vecs[1:2, :] = shift_grad


def cross_backward(
    where, x1, vec, gx2, q2, kv, p2, weights, gx1, vecs, dkv, dq2, out_mem, weight, do2, moved, sems
):
    rows, width = x1.shape
    examples = pl.num_programs(0)
    e = pl.program_id(0)
    length = p2.shape[2] // TOGETHER

    @pl.when(e == 0)
    def _():
        wait_all(load_weight(where, weight, weights, Copies(sems)))
        do2[...] = dot_nt(gx2[...].astype(BF), weight[3]).astype(BF)

    mask = head_mask(length)
    here = rows_of(e * length, length)
    for g in range(GROUPS):
        lanes = columns(g, LANES)
        value_lanes = slice(width + g * LANES, width + (g + 1) * LANES)
        queries = stack_heads(q2[here, lanes], mask)
        grads = stack_heads(do2[here, lanes], mask)
        probs = p2[0, g]
        dp = dot_nt(grads, kv[0, :, value_lanes])
        wide = probs.astype(F32)
        row_sum = jnp.sum(wide * dp, axis=-1, keepdims=True)
        dz = (wide * (dp - row_sum)).astype(BF)
        dkv[0, :, value_lanes] = dot_tn(probs, grads).astype(BF)
        dkv[0, :, lanes] = (dot_tn(dz, queries) * SCALE).astype(BF)
        dq2[here, lanes] = (merge_heads(dot(dz, kv[0, :, lanes]), mask) * SCALE).astype(BF)
    back = dot_nt(dkv[0, :, :width], weight[1]) + dot_nt(dkv[0, :, width:], weight[2])
    moved[...] = back.astype(BF)
    for d, out in enumerate(out_mem):
        slots = out.shape[1]
        out[0] = moved[rows_of((where[3] ^ d) * slots, slots), :]

    @pl.when(e == examples - 1)
    def _():
        hat, scale = normalise(x1[...])
        back, gain_grad, shift_grad = norm_back(
            dot_nt(dq2[...], weight[0]), vec[2:3, :], hat, scale
        )
        gx1[...] = gx2[...] + back
        vecs[0:1, :] = gain_grad
        vecs[1:2, :] = shift_grad


def cross_grads(
    where, gx2, a2, o2, dq2, dkv, all_memory, near, far, theirs, grad, memory, sems
):
    rows, width = gx2.shape
    examples, total, _ = memory.shape
    mem, _, slots, _ = all_memory.shape
    copies = Copies(sems)
    loads = [
        copies.start(all_memory.at[d], memory.at[:, d * slots : (d + 1) * slots, :])
        for d in range(mem)
    ]
    grad[0] = dot_tn(a2[...], dq2[...]).astype(BF)
    grad[3] = dot_tn(o2[...], gx2[...].astype(BF)).astype(BF)
    wait_all(loads)
    flat = memory[...].reshape(examples * total, width)
    for j in range(2):
        part = dkv[:, :, columns(j, width)].reshape(examples * total, width)
        grad[1 + j] = dot_tn(flat, part).astype(BF)
    wait_all(store_grad(where, grad, near, far, theirs, Copies(sems)))


def self_backward(
    group, where, suffix, vec, gx1, a1, qkv, p1, o1, parts, weights, suffix_grad, vecs,
    near, far, theirs, weight, start, grad, dqkv, do1, sems,
):
    rows, width = gx1.shape
    copies = Copies(sems)
    start_copy = my_examples(where, suffix, start, copies)
    loads = load_weight(where, weight, weights, copies)
    gs = gx1[...].astype(BF)
    grad[3] = dot_tn(o1[...], gs).astype(BF)
    wait_all(loads)
    do1[...] = dot_nt(gs, weight[3]).astype(BF)
    mask = head_mask(group)
    for r in range(rows // group):
        here = columns(r, group)
        for g in range(GROUPS):
            lanes = [slice(i * width + g * LANES, i * width + (g + 1) * LANES) for i in range(3)]
            queries = stack_heads(qkv[here, lanes[0]], mask)
            grads = stack_heads(do1[here, lanes[0]], mask)
            probs = p1[r * GROUPS + g]
            dp = dot_nt(grads, qkv[here, lanes[2]])
            wide = probs.astype(F32)
            row_sum = jnp.sum(wide * dp, axis=-1, keepdims=True)
            dz = (wide * (dp - row_sum)).astype(BF)
            dqkv[here, lanes[2]] = dot_tn(probs, grads).astype(BF)
            dqkv[here, lanes[1]] = (dot_tn(dz, queries) * SCALE).astype(BF)
            dq = merge_heads(dot(dz, qkv[here, lanes[1]]), mask) * SCALE
            dqkv[here, lanes[0]] = dq.astype(BF)
    for j in range(3):
        grad[j] = dot_tn(a1[...], dqkv[:, columns(j, width)]).astype(BF)
    start_copy.wait()
    started = store_grad(where, grad, near, far, theirs, Copies(sems))
    da1 = dot_nt(dqkv[:, columns(0, width)], weight[0])
    for j in range(1, 3):
        da1 = da1 + dot_nt(dqkv[:, columns(j, width)], weight[j])
    hat, scale = normalise(start[...].reshape(rows, width).astype(F32))
    back, gain_grad, shift_grad = norm_back(da1, vec[0:1, :], hat, scale)
    suffix_grad[...] = (gx1[...] + back).astype(BF).reshape(suffix_grad.shape)
    found = [gain_grad, shift_grad]
    for ref in parts:
        for r in range(ref.shape[0]):
            found += [ref[r : r + 1, columns(j, width)] for j in range(ref.shape[1] // width)]
    found.append(jnp.zeros((vecs.shape[0] - len(found), width), F32))
    vecs[...] = jnp.concatenate(found, axis=0).astype(BF)
    wait_all(started)


def run(kernel, inputs, outputs, scratch, copies, grid=()):
    def leaf(x):
        return isinstance(x, tuple) and len(x) == 2 and isinstance(x[0], pl.BlockSpec)

    flat_in, tree_in = jax.tree.flatten(inputs, is_leaf=leaf)
    flat_out, tree_out = jax.tree.flatten(outputs, is_leaf=leaf)

    def body(*refs):
        first, second = len(flat_in), len(flat_in) + len(flat_out)
        given = jax.tree.unflatten(tree_in, refs[:first])
        taken = jax.tree.unflatten(tree_out, refs[first:second])
        kernel(*given, *taken, *refs[second:])

    found = pl.pallas_call(
        body,
        grid=grid,
        in_specs=[spec for spec, _ in flat_in],
        out_specs=[spec for spec, _ in flat_out],
        out_shape=[shape for _, shape in flat_out],
        scratch_shapes=scratch + [pltpu.SemaphoreType.DMA((copies,))],
        compiler_params=pltpu.CompilerParams(vmem_limit_bytes=56 * 1024 * 1024),
        cost_estimate=pl.CostEstimate(
            flops=0, bytes_accessed=0, transcendentals=0
        ),
    )(*[x for _, x in flat_in])
    return jax.tree.unflatten(tree_out, found)


def shape_of(dims, dtype):
    return jax.ShapeDtypeStruct(tuple(dims), dtype)


def over_slow(value, slow, fast):
    groups = [[k * fast + b for k in range(slow)] for b in range(fast)]
    return lax.all_to_all(value, "fsdp", 0, 0, axis_index_groups=groups, tiled=True)


class Gather:
    def __init__(self, half, slow, fast):
        self.half, self.slow, self.fast = half, slow, fast

    def send_slow(self, *others):
        half = after(self.half, *others)
        self.came = [half] + [swap(half, "fsdp", k * self.fast) for k in range(1, self.slow)]

    def send_fast(self, *others):
        self.near = jnp.stack([after(piece, *others) for piece in self.came])
        self.near_other = swap(self.near, "mem", 1)
        self.far = [swap(self.near, "fsdp", b) for b in range(1, self.fast)]

    def whole(self):
        mine = [self.near] + self.far
        theirs = [self.near_other] + [swap(piece, "mem", 1) for piece in self.far]
        return mine, theirs

    @staticmethod
    def refs(weights):
        return [[(ANY, x) for x in some] for some in weights]


class Scatter:
    def __init__(self, grads, slow, fast, *others, vectors=None):
        self.near, self.far, theirs = grads
        self.slow, self.fast, self.vectors = slow, fast, vectors
        theirs = [after(part, *others) for part in theirs]
        far = [swap(part, "mem", 1) for part in theirs[1:]]
        far = [jnp.concatenate(far[2 * b : 2 * b + 2]) for b in range(fast - 1)]
        self.sent = [swap(theirs[0], "mem", 1)] + far
        if vectors is not None:
            self.vectors = vectors.astype(F32) + swap(vectors, "mem", 1).astype(F32)

    def add_cores(self):
        self.out = [
            (self.far[b].astype(F32) + self.sent[b + 1].astype(F32)).astype(BF)
            for b in range(self.fast - 1)
        ]
        return self.out

    def send_fast(self):
        self.came = [swap(part, "fsdp", b + 1) for b, part in enumerate(self.out)]
        if self.vectors is not None:
            low = self.vectors.astype(BF)
            came = [swap(low, "fsdp", b) for b in range(1, self.fast)]
            self.vectors = sum(part.astype(F32) for part in [low, *came])

    def add_fast(self, *others):
        total = after(self.near, *others).astype(F32) + self.sent[0].astype(F32)
        for part in self.came:
            total = total + part.astype(F32)
        self.total = total.astype(BF).reshape(self.slow, -1, total.shape[-1])
        if self.vectors is not None:
            low = self.vectors.astype(BF)
            low = jnp.broadcast_to(low, (self.slow,) + low.shape)
            self.total = jnp.concatenate([self.total, low], axis=1)
        return self.total

    def send_slow(self):
        self.came = over_slow(self.total, self.slow, self.fast)

    def add_slow(self, *others):
        return jnp.sum(after(self.came, *others).astype(F32), axis=0)


class Replicas:
    def __init__(self, value, rows, across):
        self.rows = rows
        k = 1
        while 2 * k < across:
            low = value.astype(BF)
            value = low.astype(F32) + swap(low, "mem", 2 * k).astype(F32)
            k *= 2
        low = value.astype(BF)
        self.halves = [low, swap(low, "mem", 2 * k)] if across > 1 else [low]

    def swap_cores(self, *others):
        halves, _ = lax.optimization_barrier((self.halves, others))
        self.others = [swap(half[: 2 * self.rows], "mem", 1) for half in halves]

    def combine(self, c):
        rows = self.rows
        other = sum(half.astype(F32) for half in self.others)
        mine = sum(half.astype(F32) for half in self.halves)
        vectors, mine = mine[2 * rows :], mine[: 2 * rows]
        first = jnp.where(c == 0, mine, other)
        second = jnp.where(c == 0, other, mine)
        return [first[:rows], first[rows:], second[:rows], second[rows:]], vectors


def place_rows(where, blocks, outs, scratch, sems):
    copies = Copies(sems)
    loads = []
    for i, (even, odd) in enumerate(blocks):
        for d, piece in enumerate(even):
            loads.append((copies.start(piece, scratch.at[i, 2 * d]), i, 2 * d))
            loads.append((copies.start(odd.at[d], scratch.at[i, 2 * d + 1]), i, 2 * d + 1))
    examples = scratch.shape[2]
    stores = []
    for load, i, d in loads:
        load.wait()
        target = outs[i].at[pl.ds((where[3] ^ d) * examples, examples)]
        stores.append(copies.start(scratch.at[i, d], target))
    wait_all(stores)


def place_memory(where, pieces, out, scratch, sems):
    examples = pieces[0].shape[0]
    copies = Copies(sems)
    loads = [copies.start(piece, scratch.at[d]) for d, piece in enumerate(pieces)]
    stores = []
    for d, load in enumerate(loads):
        load.wait()
        target = out.at[pl.ds((where[3] ^ d) * examples, examples)]
        stores.append(copies.start(scratch.at[d], target))
    wait_all(stores)


def spread_across(value, mem):
    return [value] + [swap(value, "mem", d) for d in range(2, mem, 2)]


def per_device(
    suffix,
    memory,
    counts,
    cotangent,
    self_norm_gain,
    self_norm_bias,
    self_query,
    self_key,
    self_value,
    self_output,
    cross_norm_gain,
    cross_norm_bias,
    cross_query,
    cross_key,
    cross_value,
    cross_output,
    dense_norm_gain,
    dense_norm_bias,
    dense_in,
    dense_in_bias,
    dense_out,
    dense_out_bias,
):
    f = lax.axis_index("fsdp")
    m = lax.axis_index("mem")
    c = m % 2
    fsdp = lax.axis_size("fsdp")
    mem = lax.axis_size("mem")
    across = mem // 2
    slow, fast = fsdp_split(fsdp)
    SHARDS[0] = fsdp
    where = jnp.stack([f // fast, f % fast, c, m]).astype(jnp.int32)
    examples = suffix.shape[0] // mem
    length = suffix.shape[1]
    width = suffix.shape[2]
    slots = memory.shape[1]
    total = mem * slots
    rows = examples * length
    inner = dense_in.shape[1]
    part = width // fsdp
    group = min(128, rows)
    blocks = 4 * fsdp

    def gather(matrices, *others):
        halves = [jnp.concatenate(matrices[:2]), jnp.concatenate(matrices[2:])]
        half = jnp.concatenate([jnp.where(c == 0, *halves), *others])
        return Gather(half, slow, fast)

    cross_gather = gather([cross_query, cross_key, cross_value, cross_output])
    in_gather = gather([dense_in[:, columns(j, width)] for j in range(4)])
    out_gather = gather([dense_out[columns(j, part)] for j in range(4)])
    small = [
        self_norm_gain,
        self_norm_bias,
        cross_norm_gain,
        cross_norm_bias,
        dense_norm_gain,
        dense_norm_bias,
        dense_out_bias,
    ]
    small += [dense_in_bias[columns(j, part)] for j in range(4)]
    small = sum(
        jnp.pad(value[None], ((i, 15 - i), (0, width - part))) for i, value in enumerate(small)
    )
    self_gather = gather([self_query, self_key, self_value, self_output], small)

    def exchange(value):
        blocks = value.reshape((mem, examples) + value.shape[1:])
        return lax.all_to_all(blocks, "mem", 0, 0, tiled=True)

    all_memory = exchange(memory)
    self_gather.send_slow()
    sent = self_gather.came
    self_gather.send_fast(*sent)
    cross_gather.send_slow(*sent)
    sent = [*self_gather.far, *cross_gather.came, all_memory]
    self_gather.far = [after(piece, *sent) for piece in self_gather.far]
    self_weights = self_gather.whole()
    cross_gather.send_fast(*self_gather.far)
    in_gather.send_slow(*self_gather.far)

    half = (2, part, width)
    grads_like = [
        (ANY, shape_of((slow,) + half, BF)),
        (ANY, shape_of((fast - 1, slow) + half, BF)),
        [(ANY, shape_of((slow,) + half, BF))]
        + [(ANY, shape_of((slow // 2,) + half, BF))] * (2 * fast - 2),
    ]

    def flat(dims, dtype):
        return (VMEM, shape_of(dims, dtype))

    def per_example(value):
        dims = value.shape[1:]
        spec = pl.BlockSpec((1,) + dims, lambda e: (e,) + (0,) * len(dims))
        return (spec, value)

    def slots_of_example(value):
        spec = pl.BlockSpec((mem, 1, slots, width), lambda e: (0, e, 0, 0))
        return (spec, value)

    def scratch(*dims):
        return pltpu.VMEM(dims, BF)

    def scatter(grads, *others, vectors=None):
        return Scatter(grads, slow, fast, *others, vectors=vectors)

    wide = (rows, width)
    square = scratch(4, width, width)
    own_rows = scratch(examples, length, width)
    x1, a1, qkv, p1, o1, vec = run(
        functools.partial(self_forward, group),
        [(SMEM, where), (ANY, suffix), Gather.refs(self_weights)],
        [
            flat(wide, F32),
            flat(wide, BF),
            flat((rows, 3 * width), BF),
            flat((rows // group * GROUPS, TOGETHER * group, group), BF),
            flat(wide, BF),
            flat((16, width), F32),
        ],
        [square, own_rows, scratch(fsdp, 16, 128)],
        1 + fsdp + blocks,
    )
    cross_gather.far = [after(piece, x1, *in_gather.came) for piece in cross_gather.far]
    cross_weights = Gather.refs(cross_gather.whole())
    in_gather.send_fast(*cross_gather.far)
    out_gather.send_slow(*cross_gather.far)
    x2, a2, q2, kv, p2, o2 = run(
        cross_forward,
        [(SMEM, where), (SMEM, counts), (VMEM, x1), (VMEM, vec)]
        + [slots_of_example(all_memory), cross_weights],
        [
            flat(wide, F32),
            flat(wide, BF),
            flat(wide, BF),
            per_example(shape_of((examples, total, 2 * width), BF)),
            per_example(shape_of((examples, GROUPS, TOGETHER * length, total), BF)),
            flat(wide, BF),
        ],
        [square],
        blocks,
        (examples,),
    )
    small = [after(piece, x1)[:, 2 * part + 7 : 2 * part + 11, :part] for piece in self_weights[0]]
    order = jnp.arange(fsdp) ^ f
    bias_in = jnp.take(jnp.concatenate(small), order % fast * slow + order // fast, axis=0)
    bias_in = bias_in.astype(F32).reshape(1, inner)
    in_gather.far = [after(piece, x2, *out_gather.came) for piece in in_gather.far]
    in_weights = Gather.refs(in_gather.whole())
    out_gather.send_fast(*in_gather.far)
    a3, h, slope, *grads = run(
        dense_inner,
        [(SMEM, where), (VMEM, x2), (VMEM, vec), (VMEM, bias_in), (ANY, cotangent), in_weights],
        [flat(wide, BF), flat((rows, inner), BF), flat((rows, inner), BF)] + grads_like,
        [square, scratch(fsdp, 4, part, width), own_rows],
        1 + blocks,
    )
    out_gather.far = [after(piece, a3) for piece in out_gather.far]
    out_weights = Gather.refs(out_gather.whole())
    out_scatter = scatter(grads, *out_gather.far)
    out_sum = out_scatter.add_cores()
    out_scatter.send_fast()
    y, du, vecs_y, bias_grad, *grads = run(
        dense_outer,
        [(SMEM, where), (VMEM, after(x2, *out_sum)), (VMEM, vec), (VMEM, a3), (VMEM, h)]
        + [(VMEM, slope), (ANY, cotangent), out_weights],
        [
            flat((examples, length, width), BF),
            flat((rows, inner), BF),
            flat((1, width), F32),
            flat((1, inner), F32),
        ]
        + grads_like,
        [scratch(fsdp, 4, part, width), square, own_rows],
        1 + blocks,
    )
    in_grads = grads
    gx2, vecs_dense = run(
        dense_back,
        [(SMEM, where), (VMEM, x2), (VMEM, vec), (VMEM, du), (ANY, cotangent), in_weights],
        [flat(wide, F32), flat((2, width), F32)],
        [square, own_rows],
        1 + blocks,
    )
    in_scatter = scatter(in_grads, gx2)
    in_sum = in_scatter.add_cores()
    in_scatter.send_fast()
    out_total = out_scatter.add_fast(*in_sum)
    out_scatter.send_slow()
    gx1, vecs_cross, dkv, dq2, grad_memory = run(
        cross_backward,
        [(SMEM, where), (VMEM, x1), (VMEM, vec), (VMEM, after(gx2, out_total, *in_sum)), (VMEM, q2)]
        + [per_example(kv), per_example(p2), cross_weights],
        [
            flat(wide, F32),
            flat((2, width), F32),
            per_example(shape_of((examples, total, 2 * width), BF)),
            flat(wide, BF),
            [per_example(shape_of((examples, slots, width), BF))] * mem,
        ],
        [square, scratch(*wide), scratch(total, width)],
        blocks,
        (examples,),
    )
    out_final = out_scatter.add_slow(gx1)
    mem_pieces = grad_memory[:1] + [swap(grad_memory[d], "mem", d) for d in range(1, mem)]
    grads = run(
        cross_grads,
        [(SMEM, where), (VMEM, after(gx2, out_final)), (VMEM, a2), (VMEM, o2), (VMEM, dq2)]
        + [(VMEM, dkv), (ANY, all_memory)],
        grads_like,
        [square, scratch(examples, total, width)],
        max(mem, blocks),
    )
    in_total = in_scatter.add_fast()
    in_scatter.send_slow()
    cross_scatter = scatter(grads, in_total, *mem_pieces[1:3])
    cross_sum = cross_scatter.add_cores()
    cross_scatter.send_fast()
    gx1 = after(gx1, *cross_sum)
    suffix_part, vecs_self, *grads = run(
        functools.partial(self_backward, group),
        [(SMEM, where), (ANY, suffix), (VMEM, vec), (VMEM, gx1), (VMEM, a1)]
        + [(VMEM, qkv), (VMEM, p1), (VMEM, o1)]
        + [[(VMEM, x) for x in (vecs_cross, vecs_dense, vecs_y, bias_grad)], Gather.refs(self_weights)],
        [flat((examples, length, width), BF), flat((16, width), BF)] + grads_like,
        [square, own_rows, square, scratch(rows, 3 * width), scratch(*wide)],
        1 + blocks,
    )
    in_final = in_scatter.add_slow(suffix_part)
    cross_total = cross_scatter.add_fast(suffix_part)
    cross_scatter.send_slow()
    self_scatter = scatter(grads, in_final, cross_total, vectors=vecs_self)
    self_sum = self_scatter.add_cores()
    self_scatter.send_fast()
    dense_sum = after(jnp.concatenate([out_final, in_final]), *self_sum)
    dense_sum = Replicas(dense_sum, 2 * part, across)
    y_rows = spread_across(after(y, *self_sum), mem)
    self_total = self_scatter.add_fast(*dense_sum.halves, *y_rows)
    self_scatter.send_slow()
    cross_sum = Replicas(cross_scatter.add_slow(self_total), part, across)
    suffix_rows = spread_across(after(suffix_part, self_total), mem)
    y_rows = [after(value, self_total) for value in y_rows]
    y_far = swap(jnp.stack(y_rows), "mem", 1)
    dense_sum.swap_cores(self_total)
    mem_pieces = [after(value, self_total) for value in mem_pieces]
    (memory_grad,) = run(
        place_memory,
        [(SMEM, where), [(ANY, value) for value in mem_pieces]],
        [(ANY, shape_of(memory.shape, BF))],
        [scratch(mem, examples, slots, width)],
        2 * mem,
    )
    cross_sum.swap_cores()
    suffix_far = swap(jnp.stack(suffix_rows), "mem", 1)
    blocks = [([(ANY, x) for x in y_rows], (ANY, y_far))]
    blocks += [([(ANY, x) for x in suffix_rows], (ANY, suffix_far))]
    ((block_output, suffix_grad),) = run(
        place_rows,
        [(SMEM, where), blocks],
        [[(ANY, shape_of(suffix.shape, BF))] * 2],
        [scratch(2, mem, examples, length, width)],
        4 * mem,
    )
    (out_low, in_low, out_high, in_high), _ = dense_sum.combine(c)
    grad_in = jnp.concatenate([in_low[:part], in_low[part:], in_high[:part], in_high[part:]], axis=1)
    grad_out = jnp.concatenate([out_low, out_high])
    grad_cross, _ = cross_sum.combine(c)
    done = [grad_in, grad_out, *grad_cross, block_output, memory_grad]
    self_final = Replicas(self_scatter.add_slow(*done), part, across)
    self_final.swap_cores()
    grad_self, vectors = self_final.combine(c)

    def vector(i):
        return lax.dynamic_slice(vectors, (i, f * part), (1, part)).reshape(part)

    return (
        block_output,
        suffix_grad,
        memory_grad,
        vector(0),
        vector(1),
        *grad_self,
        vector(2),
        vector(3),
        *grad_cross,
        vector(4),
        vector(5),
        grad_in,
        lax.dynamic_slice_in_dim(vectors[7:11].reshape(-1), f * (inner // fsdp), inner // fsdp, 0),
        grad_out,
        vector(6),
    )


def solution(mesh):
    rows = P("fsdp", None, None)
    matrix = P("fsdp", None)
    vector = P("fsdp")
    attention = (vector, vector, matrix, matrix, matrix, matrix)
    params = attention + attention + (vector, vector, matrix, vector, matrix, vector)
    return jax.shard_map(
        per_device,
        mesh=mesh,
        in_specs=(rows, P("fsdp", "mem", None), vector, rows) + params,
        out_specs=(rows, rows, P("fsdp", "mem", None)) + params,
        check_vma=False,
    )
```

profile of v0, /device:TPU:0, one launch (start us, length us, event | category | flops | bytes accessed | tf_op | source)
XLA Modules:
  0.0 401.4 jit_solution(5133897246902705824)
XLA Ops:
  0.8 4.4 %all-to-all-start = ((bf16[4,8,64,768]{3,2,1,0:T(8,128)(2,1)}), bf16[4,8,64,768]{3,2,1,0:T(8,128)(2,1)S(1)}, u32[]{:S(2)}, u32[]{:S(2)}) async-start(bf16[4,8,64,768]{3,2,1,0:T(8,128)(2,1)} %bitcast.73), calls=%async_computation | async-start | bytes 6291456 | tf_op jit(solution)/shard_map/all_to_all | solution.py:674
  6.4 2.6 collective-permute-start
  9.0 2.6 collective-permute-start.1
  11.6 12.0 %collective-permute-done = bf16[208,768]{1,0:T(8,128)(2,1)S(1)} collective-permute-done((bf16[208,768]{1,0:T(8,128)(2,1)S(1)}, bf16[208,768]{1,0:T(8,128)(2,1)S(1)}, u32[]{:S(2)}, u32[]{:S(2)}) %collective-permute-start) | collective-permute-done | bytes 319520 | tf_op jit(solution)/shard_map/ppermute | solution.py:25
  23.5 10.5 %collective-permute-done.1 = bf16[208,768]{1,0:T(8,128)(2,1)S(1)} collective-permute-done((bf16[208,768]{1,0:T(8,128)(2,1)S(1)}, bf16[208,768]{1,0:T(8,128)(2,1)S(1)}, u32[]{:S(2)}, u32[]{:S(2)}) %collective-permute-start.1) | collective-permute-done | bytes 319520 | tf_op jit(solution)/shard_map/ppermute | solution.py:25
  34.0 1.2 pad_maximum_fusion.refs_2_.refs_12_
  35.2 1.6 collective-permute-start.3
  37.1 6.7 %collective-permute-start.4 = (bf16[192,768]{1,0:T(8,128)(2,1)S(1)}, bf16[192,768]{1,0:T(8,128)(2,1)S(1)}, u32[]{:S(2)}, u32[]{:S(2)}) collective-permute-start(bf16[192,768]{1,0:T(8,128)(2,1)S(1)} %get-tuple-element.145), channel_id=1, source_target_pairs={{0,8},{4,12},{8,0},{12,4},{16,24},{20,28},{24,16},{28,20},{1,9},{5... | collective-permute-start | bytes 884744 | tf_op jit(solution)/shard_map/ppermute | solution.py:25
  44.9 1.4 collective-permute-start.6
  46.2 8.9 %collective-permute-done.4 = bf16[192,768]{1,0:T(8,128)(2,1)S(1)} collective-permute-done((bf16[192,768]{1,0:T(8,128)(2,1)S(1)}, bf16[192,768]{1,0:T(8,128)(2,1)S(1)}, u32[]{:S(2)}, u32[]{:S(2)}) %collective-permute-start.4) | collective-permute-done | bytes 294944 | tf_op jit(solution)/shard_map/ppermute | solution.py:25
  55.2 12.1 %collective-permute-done.5 = bf16[192,768]{1,0:T(8,128)(2,1)S(1)} collective-permute-done((bf16[192,768]{1,0:T(8,128)(2,1)S(1)}, bf16[192,768]{1,0:T(8,128)(2,1)S(1)}, u32[]{:S(2)}, u32[]{:S(2)}) %collective-permute-start.5) | collective-permute-done | bytes 294944 | tf_op jit(solution)/shard_map/ppermute | solution.py:25
  68.8 3.3 pad_maximum_fusion.2.refs_5_.refs_7_
  73.0 4.3 %collective-permute-start.10 = (bf16[192,768]{1,0:T(8,128)(2,1)S(1)}, bf16[192,768]{1,0:T(8,128)(2,1)}, u32[]{:S(2)}, u32[]{:S(2)}) collective-permute-start(bf16[192,768]{1,0:T(8,128)(2,1)S(1)} %get-tuple-element.154), channel_id=1, source_target_pairs={{0,8},{4,12},{8,0},{12,4},{16,24},{20,28},{24,16},{28,20},{1,9},{5... | collective-permute-start | bytes 884744 | tf_op jit(solution)/shard_map/ppermute | solution.py:25
  78.3 1.5 collective-permute-start.12
  80.3 7.7 %shard_map.373 = (f32[256,768]{1,0:T(8,128)}, bf16[256,768]{1,0:T(8,128)(2,1)}, bf16[256,2304]{1,0:T(8,128)(2,1)}, bf16[6,512,128]{2,1,0:T(8,128)(2,1)}, bf16[256,768]{1,0:T(8,128)(2,1)}, /*index=5*/f32[16,768]{1,0:T(8,128)}) custom-call(s32[4]{0:T(128)} %pad_add_fusion.1.refs_0_, bf16[32,32,768]{2,1,0:T(8,128)(2,1)} %refs_1_.5, ...), custom_call_target="tpu_custom_call" | custom-call | tf_op jit(solution)/shard_map/pallas_call | solution.py:458
  88.0 1.1 collective-permute-done.10
  89.1 11.7 %collective-permute-done.11 = bf16[192,768]{1,0:T(8,128)(2,1)} collective-permute-done((bf16[192,768]{1,0:T(8,128)(2,1)S(1)}, bf16[192,768]{1,0:T(8,128)(2,1)}, u32[]{:S(2)}, u32[]{:S(2)}) %collective-permute-start.11) | collective-permute-done | bytes 294944 | tf_op jit(solution)/shard_map/ppermute | solution.py:25
  100.9 1.4 pad_maximum_fusion.3.refs_5_
  103.1 5.0 %collective-permute-start.16 = (bf16[192,768]{1,0:T(8,128)(2,1)S(1)}, bf16[192,768]{1,0:T(8,128)(2,1)S(1)}, u32[]{:S(2)}, u32[]{:S(2)}) collective-permute-start(bf16[192,768]{1,0:T(8,128)(2,1)S(1)} %slice_select_fusion), channel_id=1, source_target_pairs={{0,8},{4,12},{8,0},{12,4},{16,24},{20,28},{24,16},{28,20},{1,9},{5... | collective-permute-start | bytes 884744 | tf_op jit(solution)/shard_map/ppermute | solution.py:25
  109.2 1.4 collective-permute-start.18
  111.7 16.7 %shard_map.374 = (f32[256,768]{1,0:T(8,128)}, bf16[256,768]{1,0:T(8,128)(2,1)}, bf16[256,768]{1,0:T(8,128)(2,1)}, bf16[8,256,1536]{2,1,0:T(8,128)(2,1)}, bf16[8,...) custom-call(s32[4]{0:T(128)} %pad_add_fusion.1.refs_0_, s32[32]{0:T(128)} %refs_1_.4, ...), custom_call_target="tpu_custom_call" | custom-call | tf_op jit(solution)/shard_map/pallas_call | solution.py:458
  128.4 3.2 collective-permute-done.17
  131.6 1.3 pad_maximum_fusion.4.refs_7_
  133.0 1.2 collective-permute-start.21
  136.2 1.2 gather_fusion
  139.9 13.6 %shard_map.375 = (bf16[256,768]{1,0:T(8,128)(2,1)}, bf16[256,3072]{1,0:T(8,128)(2,1)}, bf16[256,3072]{1,0:T(8,128)(2,1)}, bf16[4,2,96,768]{3,2,1,0:T(8,128)(2,1)...) custom-call(s32[4]{0:T(128)} %pad_add_fusion.1.refs_0_, ...), custom_call_target="tpu_custom_call" | custom-call | tf_op jit(solution)/shard_map/pallas_call | solution.py:458
  153.5 8.0 %collective-permute-done.21.refs_8_ = bf16[4,192,768]{2,1,0:T(8,128)(2,1)} collective-permute-done((bf16[4,192,768]{2,1,0:T(8,128)(2,1)}, bf16[4,192,768]{2,1,0:T(8,128)(2,1)}, u32[]{:S(2)}, u32[]{:S(2)}) %collective-permute-start.21) | collective-permute-done | bytes 1179680 | tf_op jit(solution)/shard_map/ppermute | solution.py:25
  162.5 2.9 collective-permute-done.22
  166.2 1.5 fusion.3
  167.8 1.3 collective-permute-start.29
  170.5 11.8 %shard_map.376 = (bf16[8,32,768]{2,1,0:T(8,128)(2,1)}, bf16[256,3072]{1,0:T(8,128)(2,1)}, f32[1,768]{1,0:T(1,128)}, f32[1,3072]{1,0:T(1,128)}, bf16[4,2,96,768]{...) custom-call(s32[4]{0:T(128)} %pad_add_fusion.1.refs_0_, ...), custom_call_target="tpu_custom_call" | custom-call | tf_op jit(solution)/shard_map/pallas_call | solution.py:458
  182.3 7.3 %shard_map.377 = (f32[256,768]{1,0:T(8,128)}, f32[2,768]{1,0:T(2,128)}) custom-call(s32[4]{0:T(128)} %pad_add_fusion.1.refs_0_, f32[256,768]{1,0:T(8,128)} %get-tuple-element.171.refs_1_, f32[16,768]{1,0:T(8,128)} %get-tuple-element.144.refs_3_.refs_2_, bf16[256,3072]{1,0:T(8,128)(2,1)} %get-tuple-element.175.refs_3_, bf16[32,32,768]{2,1,0:T(8,128)(2,1)} %refs_4_.3, ...), custom_call_target="tpu_custom_call" | custom-call | tf_op jit(solution)/shard_map/pallas_call | solution.py:458
  190.2 1.5 collective-permute-done.26
  192.9 3.0 collective-permute-done.29
  195.9 1.5 add_convert_fusion.3
  197.4 8.1 %all-to-all-start.1 = ((bf16[4,192,768]{2,1,0:T(8,128)(2,1)}), bf16[4,192,768]{2,1,0:T(8,128)(2,1)S(1)}, u32[]{:S(2)}, u32[]{:S(2)}) async-start(bf16[4,192,768]{2,1,0:T(8,128)(2,1)} %bitcast.35), calls=%async_computation.1 | async-start | bytes 2359296 | tf_op jit(solution)/shard_map/all_to_all | solution.py:479
  205.5 1.2 collective-permute-start.31
  206.7 23.3 %shard_map.378 = (f32[256,768]{1,0:T(8,128)}, f32[2,768]{1,0:T(2,128)}, bf16[8,256,1536]{2,1,0:T(8,128)(2,1)}, bf16[256,768]{1,0:T(8,128)(2,1)}, bf16[8,64,768]{...) custom-call(s32[4]{0:T(128)} %pad_add_fusion.1.refs_0_, ...), custom_call_target="tpu_custom_call" | custom-call | tf_op jit(solution)/shard_map/pallas_call | solution.py:458
  230.3 1.4 collective-permute-start.33
  231.7 2.2 collective-permute-done.31
  233.9 1.5 add_convert_fusion.2
  236.2 12.8 %shard_map.379 = (bf16[4,2,96,768]{3,2,1,0:T(8,128)(2,1)}, bf16[1,4,2,96,768]{4,3,2,1,0:T(8,128)(2,1)}, bf16[4,2,96,768]{3,2,1,0:T(8,128)(2,1)}, bf16[2,2,96,768]{3,2,1,0:T(8,128)(2,1)}, bf16[2,2,96,768]{3,2,1,0:T(8,128)(2,1)}) custom-call(s32[4]{0:T(128)} %pad_add_fusion.1.refs_0_, f32[256,768]{1,0:T(8,128)} %get-tuple-element.192.refs_3_.refs_1_, ...), custom_call_target="tpu_custom_call" | custom-call | tf_op jit(solution)/shard_map/pallas_call | solution.py:458
  249.0 1.3 collective-permute-done.33.refs_3_
  250.9 5.3 %all-to-all-start.2 = ((bf16[4,192,768]{2,1,0:T(8,128)(2,1)}), bf16[4,192,768]{2,1,0:T(8,128)(2,1)S(1)}, u32[]{:S(2)}, u32[]{:S(2)}) async-start(bf16[4,192,768]{2,1,0:T(8,128)(2,1)} %bitcast.37), calls=%async_computation.2 | async-start | bytes 2359296 | tf_op jit(solution)/shard_map/all_to_all | solution.py:479
  257.2 1.5 fusion.1
  259.6 11.7 %shard_map.380 = (bf16[8,32,768]{2,1,0:T(8,128)(2,1)}, bf16[16,768]{1,0:T(8,128)(2,1)}, bf16[4,2,96,768]{3,2,1,0:T(8,128)(2,1)}, bf16[1,4,2,96,768]{4,3,2,1,0:T(...) custom-call(s32[4]{0:T(128)} %pad_add_fusion.1.refs_0_, ...), custom_call_target="tpu_custom_call" | custom-call | tf_op jit(solution)/shard_map/pallas_call | solution.py:458
  271.3 13.9 %all-to-all-done.2 = bf16[4,192,768]{2,1,0:T(8,128)(2,1)S(1)} async-done(((bf16[4,192,768]{2,1,0:T(8,128)(2,1)}), bf16[4,192,768]{2,1,0:T(8,128)(2,1)S(1)}, u32[]{:S(2)}, u32[]{:S(2)}) %all-to-all-start.2) | async-done | bytes 1179680 | tf_op jit(solution)/shard_map/all_to_all | solution.py:479
  286.0 1.2 collective-permute-done.37
  287.2 3.1 add_convert_fusion.1
  290.8 5.1 %all-to-all-start.4 = ((bf16[4,192,768]{2,1,0:T(8,128)(2,1)}), bf16[4,192,768]{2,1,0:T(8,128)(2,1)S(1)}, u32[]{:S(2)}, u32[]{:S(2)}) async-start(bf16[4,192,768]{2,1,0:T(8,128)(2,1)} %bitcast.39), calls=%async_computation.4 | async-start | bytes 2359296 | tf_op jit(solution)/shard_map/all_to_all | solution.py:479
  297.2 1.4 collective-permute-start.40
  299.8 1.3 collective-permute-start.45
  301.1 24.1 %collective-permute-done.45 = bf16[16,768]{1,0:T(8,128)(2,1)S(1)} collective-permute-done((bf16[16,768]{1,0:T(8,128)(2,1)S(1)}, bf16[16,768]{1,0:T(8,128)(2,1)S(1)}, u32[]{:S(2)}, u32[]{:S(2)}) %collective-permute-start.45) | collective-permute-done | bytes 24608 | tf_op jit(solution)/shard_map/ppermute | solution.py:25
  327.3 1.1 pad_maximum_fusion.1
  330.1 1.3 collective-permute-start.47
  331.5 20.1 %collective-permute-done.52 = bf16[192,768]{1,0:T(8,128)(2,1)} collective-permute-done((bf16[192,768]{1,0:T(8,128)(2,1)}, bf16[192,768]{1,0:T(8,128)(2,1)}, u32[]{:S(2)}, u32[]{:S(2)}) %collective-permute-start.52) | collective-permute-done | bytes 294944 | tf_op jit(solution)/shard_map/ppermute | solution.py:25
  352.1 5.1 %all-to-all-start.3 = ((bf16[4,208,768]{2,1,0:T(8,128)(2,1)}), bf16[4,208,768]{2,1,0:T(8,128)(2,1)S(1)}, u32[]{:S(2)}, u32[]{:S(2)}) async-start(bf16[4,208,768]{2,1,0:T(8,128)(2,1)} %pad_maximum_fusion.1), calls=%async_computation.3 | async-start | bytes 2555904 | tf_op jit(solution)/shard_map/all_to_all | solution.py:479
  357.7 3.5 shard_map.382
  362.0 1.4 fusion.6
  365.1 1.6 fusion.5
  371.7 3.4 shard_map.381
  375.2 13.0 %all-to-all-done.3 = bf16[4,208,768]{2,1,0:T(8,128)(2,1)S(1)} async-done(((bf16[4,208,768]{2,1,0:T(8,128)(2,1)}), bf16[4,208,768]{2,1,0:T(8,128)(2,1)S(1)}, u32[]{:S(2)}, u32[]{:S(2)}) %all-to-all-start.3) | async-done | bytes 1277984 | tf_op jit(solution)/shard_map/all_to_all | solution.py:479
  388.4 1.4 collective-permute-start.55
  389.9 7.2 %collective-permute-done.55 = bf16[208,768]{1,0:T(8,128)(2,1)S(1)} collective-permute-done((bf16[208,768]{1,0:T(8,128)(2,1)S(1)}, bf16[208,768]{1,0:T(8,128)(2,1)S(1)}, u32[]{:S(2)}, u32[]{:S(2)}) %collective-permute-start.55) | collective-permute-done | bytes 319520 | tf_op jit(solution)/shard_map/ppermute | solution.py:25
  (233 shorter events, 42.9 us)
Async XLA Ops:
  0.8 67.9 %all-to-all-start = ((bf16[4,8,64,768]{3,2,1,0:T(8,128)(2,1)}), bf16[4,8,64,768]{3,2,1,0:T(8,128)(2,1)S(1)}, u32[]{:S(2)}, u32[]{:S(2)}) async-start(bf16[4,8,64,768]{3,2,1,0:T(8,128)(2,1)} %bitcast.73), calls=%async_computation | async-start | bytes 6291456 | tf_op jit(solution)/shard_map/all_to_all | solution.py:674
  6.4 17.2 %collective-permute-start = (bf16[208,768]{1,0:T(8,128)(2,1)S(1)}, bf16[208,768]{1,0:T(8,128)(2,1)S(1)}, u32[]{:S(2)}, u32[]{:S(2)}) collective-permute-start(bf16[208,768]{1,0:T(8,128)(2,1)S(1)} %pad_maximum_fusion.10), channel_id=1, source_target_pairs={{0,8},{4,12},{8,0},{12,4},{16,24},{20,28},{24,16},{28,20},{1,9},{5... | collective-permute-start | bytes 958472 | tf_op jit(solution)/shard_map/ppermute | solution.py:25
  9.0 25.0 %collective-permute-start.1 = (bf16[208,768]{1,0:T(8,128)(2,1)S(1)}, bf16[208,768]{1,0:T(8,128)(2,1)S(1)}, u32[]{:S(2)}, u32[]{:S(2)}) collective-permute-start(bf16[208,768]{1,0:T(8,128)(2,1)S(1)} %pad_maximum_fusion.10), channel_id=1, source_target_pairs={{0,16},{4,20},{8,24},{12,28},{16,0},{20,4},{24,8},{28,12},{1,17},{... | collective-permute-start | bytes 958472 | tf_op jit(solution)/shard_map/ppermute | solution.py:25
  11.6 22.4 %collective-permute-start.2 = (bf16[208,768]{1,0:T(8,128)(2,1)S(1)}, bf16[208,768]{1,0:T(8,128)(2,1)S(1)}, u32[]{:S(2)}, u32[]{:S(2)}) collective-permute-start(bf16[208,768]{1,0:T(8,128)(2,1)S(1)} %pad_maximum_fusion.10), channel_id=1, source_target_pairs={{0,24},{4,28},{8,16},{12,20},{16,8},{20,12},{24,0},{28,4},{1,25},{... | collective-permute-start | bytes 958472 | tf_op jit(solution)/shard_map/ppermute | solution.py:25
  35.2 33.4 %collective-permute-start.3 = (bf16[4,208,768]{2,1,0:T(8,128)(2,1)}, bf16[4,208,768]{2,1,0:T(8,128)(2,1)}, u32[]{:S(2)}, u32[]{:S(2)}) collective-permute-start(bf16[4,208,768]{2,1,0:T(8,128)(2,1)} %pad_maximum_fusion.refs_2_.refs_12_), channel_id=1, source_target_pairs={{0,4},{4,0},{8,12},{12,8},{16,20},{20,16},{24,28},{28,24},{1,5},{5... | collective-permute-start | bytes 3833864 | tf_op jit(solution)/shard_map/ppermute | solution.py:25
  37.1 18.1 %collective-permute-start.4 = (bf16[192,768]{1,0:T(8,128)(2,1)S(1)}, bf16[192,768]{1,0:T(8,128)(2,1)S(1)}, u32[]{:S(2)}, u32[]{:S(2)}) collective-permute-start(bf16[192,768]{1,0:T(8,128)(2,1)S(1)} %get-tuple-element.145), channel_id=1, source_target_pairs={{0,8},{4,12},{8,0},{12,4},{16,24},{20,28},{24,16},{28,20},{1,9},{5... | collective-permute-start | bytes 884744 | tf_op jit(solution)/shard_map/ppermute | solution.py:25
  43.8 23.5 %collective-permute-start.5 = (bf16[192,768]{1,0:T(8,128)(2,1)S(1)}, bf16[192,768]{1,0:T(8,128)(2,1)S(1)}, u32[]{:S(2)}, u32[]{:S(2)}) collective-permute-start(bf16[192,768]{1,0:T(8,128)(2,1)S(1)} %get-tuple-element.145), channel_id=1, source_target_pairs={{0,16},{4,20},{8,24},{12,28},{16,0},{20,4},{24,8},{28,12},{1,17},{... | collective-permute-start | bytes 884744 | tf_op jit(solution)/shard_map/ppermute | solution.py:25
  44.9 22.4 %collective-permute-start.6 = (bf16[192,768]{1,0:T(8,128)(2,1)S(1)}, bf16[192,768]{1,0:T(8,128)(2,1)S(1)}, u32[]{:S(2)}, u32[]{:S(2)}) collective-permute-start(bf16[192,768]{1,0:T(8,128)(2,1)S(1)} %get-tuple-element.145), channel_id=1, source_target_pairs={{0,24},{4,28},{8,16},{12,20},{16,8},{20,12},{24,0},{28,4},{1,25},{... | collective-permute-start | bytes 884744 | tf_op jit(solution)/shard_map/ppermute | solution.py:25
  46.2 32.0 %collective-permute-start.7 = (bf16[4,208,768]{2,1,0:T(8,128)(2,1)}, bf16[4,208,768]{2,1,0:T(8,128)(2,1)}, u32[]{:S(2)}, u32[]{:S(2)}) collective-permute-start(bf16[4,208,768]{2,1,0:T(8,128)(2,1)} %pad_maximum_fusion.refs_2_.refs_12_), channel_id=1, source_target_pairs={{0,1},{1,0},{2,3},{3,2},{4,5},{5,4},{6,7},{7,6},{8,9},{9,8},{10,11... | collective-permute-start | bytes 3833864 | tf_op jit(solution)/shard_map/ppermute | solution.py:25
  68.7 11.1 %collective-permute-start.8 = (bf16[4,208,768]{2,1,0:T(8,128)(2,1)}, bf16[4,208,768]{2,1,0:T(8,128)(2,1)}, u32[]{:S(2)}, u32[]{:S(2)}) collective-permute-start(bf16[4,208,768]{2,1,0:T(8,128)(2,1)} %collective-permute-done.3.refs_3_.refs_13_), channel_id=1, source_target_pairs={{0,1},{1,0},{2,3},{3,2},{4,5},{5,4},{6,7},{7,6},{8,9},{9,8},{10,11... | collective-permute-start | bytes 3833864 | tf_op jit(solution)/shard_map/ppermute | solution.py:25
  72.1 28.8 %collective-permute-start.9 = (bf16[4,192,768]{2,1,0:T(8,128)(2,1)}, bf16[4,192,768]{2,1,0:T(8,128)(2,1)}, u32[]{:S(2)}, u32[]{:S(2)}) collective-permute-start(bf16[4,192,768]{2,1,0:T(8,128)(2,1)} %pad_maximum_fusion.2.refs_5_.refs_7_), channel_id=1, source_target_pairs={{0,4},{4,0},{8,12},{12,8},{16,20},{20,16},{24,28},{28,24},{1,5},{5... | collective-permute-start | bytes 3538952 | tf_op jit(solution)/shard_map/ppermute | solution.py:25
  73.0 16.1 %collective-permute-start.10 = (bf16[192,768]{1,0:T(8,128)(2,1)S(1)}, bf16[192,768]{1,0:T(8,128)(2,1)}, u32[]{:S(2)}, u32[]{:S(2)}) collective-permute-start(bf16[192,768]{1,0:T(8,128)(2,1)S(1)} %get-tuple-element.154), channel_id=1, source_target_pairs={{0,8},{4,12},{8,0},{12,4},{16,24},{20,28},{24,16},{28,20},{1,9},{5... | collective-permute-start | bytes 884744 | tf_op jit(solution)/shard_map/ppermute | solution.py:25
  77.3 23.6 %collective-permute-start.11 = (bf16[192,768]{1,0:T(8,128)(2,1)S(1)}, bf16[192,768]{1,0:T(8,128)(2,1)}, u32[]{:S(2)}, u32[]{:S(2)}) collective-permute-start(bf16[192,768]{1,0:T(8,128)(2,1)S(1)} %get-tuple-element.154), channel_id=1, source_target_pairs={{0,16},{4,20},{8,24},{12,28},{16,0},{20,4},{24,8},{28,12},{1,17},{... | collective-permute-start | bytes 884744 | tf_op jit(solution)/shard_map/ppermute | solution.py:25
  78.3 22.6 %collective-permute-start.12 = (bf16[192,768]{1,0:T(8,128)(2,1)S(1)}, bf16[192,768]{1,0:T(8,128)(2,1)}, u32[]{:S(2)}, u32[]{:S(2)}) collective-permute-start(bf16[192,768]{1,0:T(8,128)(2,1)S(1)} %get-tuple-element.154), channel_id=1, source_target_pairs={{0,24},{4,28},{8,16},{12,20},{16,8},{20,12},{24,0},{28,4},{1,25},{... | collective-permute-start | bytes 884744 | tf_op jit(solution)/shard_map/ppermute | solution.py:25
  79.8 29.5 %collective-permute-start.13 = (bf16[4,192,768]{2,1,0:T(8,128)(2,1)}, bf16[4,192,768]{2,1,0:T(8,128)(2,1)}, u32[]{:S(2)}, u32[]{:S(2)}) collective-permute-start(bf16[4,192,768]{2,1,0:T(8,128)(2,1)} %pad_maximum_fusion.2.refs_5_.refs_7_), channel_id=1, source_target_pairs={{0,1},{1,0},{2,3},{3,2},{4,5},{5,4},{6,7},{7,6},{8,9},{9,8},{10,11... | collective-permute-start | bytes 3538952 | tf_op jit(solution)/shard_map/ppermute | solution.py:25
  100.9 9.7 %collective-permute-start.14 = (bf16[4,192,768]{2,1,0:T(8,128)(2,1)}, bf16[4,192,768]{2,1,0:T(8,128)(2,1)S(1)}, u32[]{:S(2)}, u32[]{:S(2)}) collective-permute-start(bf16[4,192,768]{2,1,0:T(8,128)(2,1)} %collective-permute-done.9.refs_6_.refs_8_), channel_id=1, source_target_pairs={{0,1},{1,0},{2,3},{3,2},{4,5},{5,4},{6,7},{7,6},{8,9},{9,8},{10,11... | collective-permute-start | bytes 3538952 | tf_op jit(solution)/shard_map/ppermute | solution.py:25
  102.3 29.3 %collective-permute-start.15 = (bf16[4,192,768]{2,1,0:T(8,128)(2,1)S(1)}, bf16[4,192,768]{2,1,0:T(8,128)(2,1)S(1)}, u32[]{:S(2)}, u32[]{:S(2)}) collective-permute-start(bf16[4,192,768]{2,1,0:T(8,128)(2,1)S(1)} %pad_maximum_fusion.3.refs_5_), channel_id=1, source_target_pairs={{0,4},{4,0},{8,12},{12,8},{16,20},{20,16},{24,28},{28,24},{1,5},{5... | collective-permute-start | bytes 3538952 | tf_op jit(solution)/shard_map/ppermute | solution.py:25
  103.1 25.2 %collective-permute-start.16 = (bf16[192,768]{1,0:T(8,128)(2,1)S(1)}, bf16[192,768]{1,0:T(8,128)(2,1)S(1)}, u32[]{:S(2)}, u32[]{:S(2)}) collective-permute-start(bf16[192,768]{1,0:T(8,128)(2,1)S(1)} %slice_select_fusion), channel_id=1, source_target_pairs={{0,8},{4,12},{8,0},{12,4},{16,24},{20,28},{24,16},{28,20},{1,9},{5... | collective-permute-start | bytes 884744 | tf_op jit(solution)/shard_map/ppermute | solution.py:25
  108.1 23.4 %collective-permute-start.17 = (bf16[192,768]{1,0:T(8,128)(2,1)S(1)}, bf16[192,768]{1,0:T(8,128)(2,1)S(1)}, u32[]{:S(2)}, u32[]{:S(2)}) collective-permute-start(bf16[192,768]{1,0:T(8,128)(2,1)S(1)} %slice_select_fusion), channel_id=1, source_target_pairs={{0,16},{4,20},{8,24},{12,28},{16,0},{20,4},{24,8},{28,12},{1,17},{... | collective-permute-start | bytes 884744 | tf_op jit(solution)/shard_map/ppermute | solution.py:25
  109.2 22.3 %collective-permute-start.18 = (bf16[192,768]{1,0:T(8,128)(2,1)S(1)}, bf16[192,768]{1,0:T(8,128)(2,1)S(1)}, u32[]{:S(2)}, u32[]{:S(2)}) collective-permute-start(bf16[192,768]{1,0:T(8,128)(2,1)S(1)} %slice_select_fusion), channel_id=1, source_target_pairs={{0,24},{4,28},{8,16},{12,20},{16,8},{20,12},{24,0},{28,4},{1,25},{... | collective-permute-start | bytes 884744 | tf_op jit(solution)/shard_map/ppermute | solution.py:25
  110.6 28.3 %collective-permute-start.19 = (bf16[4,192,768]{2,1,0:T(8,128)(2,1)S(1)}, bf16[4,192,768]{2,1,0:T(8,128)(2,1)}, u32[]{:S(2)}, u32[]{:S(2)}) collective-permute-start(bf16[4,192,768]{2,1,0:T(8,128)(2,1)S(1)} %pad_maximum_fusion.3.refs_5_), channel_id=1, source_target_pairs={{0,1},{1,0},{2,3},{3,2},{4,5},{5,4},{6,7},{7,6},{8,9},{9,8},{10,11... | collective-permute-start | bytes 3538952 | tf_op jit(solution)/shard_map/ppermute | solution.py:25
  131.6 7.4 %collective-permute-start.20 = (bf16[4,192,768]{2,1,0:T(8,128)(2,1)S(1)}, bf16[4,192,768]{2,1,0:T(8,128)(2,1)S(1)}, u32[]{:S(2)}, u32[]{:S(2)}) collective-permute-start(bf16[4,192,768]{2,1,0:T(8,128)(2,1)S(1)} %collective-permute-done.15.refs_6_), channel_id=1, source_target_pairs={{0,1},{1,0},{2,3},{3,2},{4,5},{5,4},{6,7},{7,6},{8,9},{9,8},{10,11... | collective-permute-start | bytes 3538952 | tf_op jit(solution)/shard_map/ppermute | solution.py:25
  133.0 28.5 %collective-permute-start.21 = (bf16[4,192,768]{2,1,0:T(8,128)(2,1)}, bf16[4,192,768]{2,1,0:T(8,128)(2,1)}, u32[]{:S(2)}, u32[]{:S(2)}) collective-permute-start(bf16[4,192,768]{2,1,0:T(8,128)(2,1)} %pad_maximum_fusion.4.refs_7_), channel_id=1, source_target_pairs={{0,4},{4,0},{8,12},{12,8},{16,20},{20,16},{24,28},{28,24},{1,5},{5... | collective-permute-start | bytes 3538952 | tf_op jit(solution)/shard_map/ppermute | solution.py:25
  138.9 30.2 %collective-permute-start.24 = (bf16[4,192,768]{2,1,0:T(8,128)(2,1)}, bf16[4,192,768]{2,1,0:T(8,128)(2,1)S(1)}, u32[]{:S(2)}, u32[]{:S(2)}) collective-permute-start(bf16[4,192,768]{2,1,0:T(8,128)(2,1)} %pad_maximum_fusion.4.refs_7_), channel_id=1, source_target_pairs={{0,1},{1,0},{2,3},{3,2},{4,5},{5,4},{6,7},{7,6},{8,9},{9,8},{10,11... | collective-permute-start | bytes 3538952 | tf_op jit(solution)/shard_map/ppermute | solution.py:25
  161.5 7.6 %collective-permute-start.25 = (bf16[4,192,768]{2,1,0:T(8,128)(2,1)}, bf16[4,192,768]{2,1,0:T(8,128)(2,1)S(1)}, u32[]{:S(2)}, u32[]{:S(2)}) collective-permute-start(bf16[4,192,768]{2,1,0:T(8,128)(2,1)} %collective-permute-done.21.refs_8_), channel_id=1, source_target_pairs={{0,1},{1,0},{2,3},{3,2},{4,5},{5,4},{6,7},{7,6},{8,9},{9,8},{10,11... | collective-permute-start | bytes 3538952 | tf_op jit(solution)/shard_map/ppermute | solution.py:25
  161.5 3.9 collective-permute-start.22
  162.0 4.2 %collective-permute-start.23 = (bf16[2,2,96,768]{3,2,1,0:T(8,128)(2,1)}, bf16[2,2,96,768]{3,2,1,0:T(8,128)(2,1)S(1)}, u32[]{:S(2)}, u32[]{:S(2)}) collective-permute-start(bf16[2,2,96,768]{3,2,1,0:T(8,128)(2,1)} %get-tuple-element.170), channel_id=1, source_target_pairs={{0,1},{1,0},{2,3},{3,2},{4,5},{5,4},{6,7},{7,6},{8,9},{9,8},{10,11... | collective-permute-start | bytes 1769480 | tf_op jit(solution)/shard_map/ppermute | solution.py:25
  162.0 30.9 %collective-permute-start.28 = (bf16[4,2,96,768]{3,2,1,0:T(8,128)(2,1)}, bf16[4,2,96,768]{3,2,1,0:T(8,128)(2,1)S(1)}, u32[]{:S(2)}, u32[]{:S(2)}) collective-permute-start(bf16[4,2,96,768]{3,2,1,0:T(8,128)(2,1)} %get-tuple-element.185), channel_id=1, source_target_pairs={{0,1},{1,0},{2,3},{3,2},{4,5},{5,4},{6,7},{7,6},{8,9},{9,8},{10,11... | collective-permute-start | bytes 3538952 | tf_op jit(solution)/shard_map/ppermute | solution.py:25
  167.8 28.1 %collective-permute-start.29 = (bf16[4,2,96,768]{3,2,1,0:T(8,128)(2,1)S(1)}, bf16[4,2,96,768]{3,2,1,0:T(8,128)(2,1)S(1)}, u32[]{:S(2)}, u32[]{:S(2)}) collective-permute-start(bf16[4,2,96,768]{3,2,1,0:T(8,128)(2,1)S(1)} %fusion.3), channel_id=1, source_target_pairs={{0,4},{4,0},{8,12},{12,8},{16,20},{20,16},{24,28},{28,24},{1,5},{5... | collective-permute-start | bytes 3538952 | tf_op jit(solution)/shard_map/ppermute | solution.py:25
  189.7 2.1 collective-permute-start.26
  189.8 2.8 collective-permute-start.27
  197.4 38.0 %all-to-all-start.1 = ((bf16[4,192,768]{2,1,0:T(8,128)(2,1)}), bf16[4,192,768]{2,1,0:T(8,128)(2,1)S(1)}, u32[]{:S(2)}, u32[]{:S(2)}) async-start(bf16[4,192,768]{2,1,0:T(8,128)(2,1)} %bitcast.35), calls=%async_computation.1 | async-start | bytes 2359296 | tf_op jit(solution)/shard_map/all_to_all | solution.py:479
  205.5 26.2 %collective-permute-start.30 = (bf16[4,2,96,768]{3,2,1,0:T(8,128)(2,1)}, bf16[4,2,96,768]{3,2,1,0:T(8,128)(2,1)S(1)}, u32[]{:S(2)}, u32[]{:S(2)}) collective-permute-start(bf16[4,2,96,768]{3,2,1,0:T(8,128)(2,1)} %get-tuple-element.201), channel_id=1, source_target_pairs={{0,1},{1,0},{2,3},{3,2},{4,5},{5,4},{6,7},{7,6},{8,9},{9,8},{10,11... | collective-permute-start | bytes 3538952 | tf_op jit(solution)/shard_map/ppermute | solution.py:25
  205.5 28.4 %collective-permute-start.31 = (bf16[4,2,96,768]{3,2,1,0:T(8,128)(2,1)S(1)}, bf16[4,2,96,768]{3,2,1,0:T(8,128)(2,1)S(1)}, u32[]{:S(2)}, u32[]{:S(2)}) collective-permute-start(bf16[4,2,96,768]{3,2,1,0:T(8,128)(2,1)S(1)} %fusion.2), channel_id=1, source_target_pairs={{0,4},{4,0},{8,12},{12,8},{16,20},{20,16},{24,28},{28,24},{1,5},{5... | collective-permute-start | bytes 3538952 | tf_op jit(solution)/shard_map/ppermute | solution.py:25
  230.0 19.0 %collective-permute-start.32 = (bf16[8,64,768]{2,1,0:T(8,128)(2,1)}, bf16[8,64,768]{2,1,0:T(8,128)(2,1)S(1)}, u32[]{:S(2)}, u32[]{:S(2)}) collective-permute-start(bf16[8,64,768]{2,1,0:T(8,128)(2,1)} %get-tuple-element.202), channel_id=1, source_target_pairs={{0,1},{1,0},{2,3},{3,2},{4,5},{5,4},{6,7},{7,6},{8,9},{9,8},{10,11... | collective-permute-start | bytes 2359304 | tf_op jit(solution)/shard_map/ppermute | solution.py:25
  230.3 20.0 %collective-permute-start.33 = (bf16[8,64,768]{2,1,0:T(8,128)(2,1)}, bf16[8,64,768]{2,1,0:T(8,128)(2,1)}, u32[]{:S(2)}, u32[]{:S(2)}) collective-permute-start(bf16[8,64,768]{2,1,0:T(8,128)(2,1)} %get-tuple-element.203), channel_id=1, source_target_pairs={{0,2},{1,3},{2,0},{3,1},{4,6},{5,7},{6,4},{7,5},{8,10},{9,11},{10,... | collective-permute-start | bytes 2359304 | tf_op jit(solution)/shard_map/ppermute | solution.py:25
  250.4 5.9 %collective-permute-start.34 = (bf16[2,2,96,768]{3,2,1,0:T(8,128)(2,1)}, bf16[2,2,96,768]{3,2,1,0:T(8,128)(2,1)}, u32[]{:S(2)}, u32[]{:S(2)}) collective-permute-start(bf16[2,2,96,768]{3,2,1,0:T(8,128)(2,1)} %get-tuple-element.204), channel_id=1, source_target_pairs={{0,1},{1,0},{2,3},{3,2},{4,5},{5,4},{6,7},{7,6},{8,9},{9,8},{10,11... | collective-permute-start | bytes 1769480 | tf_op jit(solution)/shard_map/ppermute | solution.py:25
  250.4 5.9 %collective-permute-start.35 = (bf16[2,2,96,768]{3,2,1,0:T(8,128)(2,1)}, bf16[2,2,96,768]{3,2,1,0:T(8,128)(2,1)S(1)}, u32[]{:S(2)}, u32[]{:S(2)}) collective-permute-start(bf16[2,2,96,768]{3,2,1,0:T(8,128)(2,1)} %get-tuple-element.206), channel_id=1, source_target_pairs={{0,1},{1,0},{2,3},{3,2},{4,5},{5,4},{6,7},{7,6},{8,9},{9,8},{10,11... | collective-permute-start | bytes 1769480 | tf_op jit(solution)/shard_map/ppermute | solution.py:25
  250.9 34.2 %all-to-all-start.2 = ((bf16[4,192,768]{2,1,0:T(8,128)(2,1)}), bf16[4,192,768]{2,1,0:T(8,128)(2,1)S(1)}, u32[]{:S(2)}, u32[]{:S(2)}) async-start(bf16[4,192,768]{2,1,0:T(8,128)(2,1)} %bitcast.37), calls=%async_computation.2 | async-start | bytes 2359296 | tf_op jit(solution)/shard_map/all_to_all | solution.py:479
  256.2 29.8 %collective-permute-start.36 = (bf16[4,2,96,768]{3,2,1,0:T(8,128)(2,1)}, bf16[4,2,96,768]{3,2,1,0:T(8,128)(2,1)}, u32[]{:S(2)}, u32[]{:S(2)}) collective-permute-start(bf16[4,2,96,768]{3,2,1,0:T(8,128)(2,1)} %get-tuple-element.223), channel_id=1, source_target_pairs={{0,1},{1,0},{2,3},{3,2},{4,5},{5,4},{6,7},{7,6},{8,9},{9,8},{10,11... | collective-permute-start | bytes 3538952 | tf_op jit(solution)/shard_map/ppermute | solution.py:25
  258.7 28.5 %collective-permute-start.37 = (bf16[4,2,96,768]{3,2,1,0:T(8,128)(2,1)S(1)}, bf16[4,2,96,768]{3,2,1,0:T(8,128)(2,1)}, u32[]{:S(2)}, u32[]{:S(2)}) collective-permute-start(bf16[4,2,96,768]{3,2,1,0:T(8,128)(2,1)S(1)} %fusion.1), channel_id=1, source_target_pairs={{0,4},{4,0},{8,12},{12,8},{16,20},{20,16},{24,28},{28,24},{1,5},{5... | collective-permute-start | bytes 3538952 | tf_op jit(solution)/shard_map/ppermute | solution.py:25
  290.3 5.6 %collective-permute-start.38 = (bf16[2,2,96,768]{3,2,1,0:T(8,128)(2,1)}, bf16[2,2,96,768]{3,2,1,0:T(8,128)(2,1)S(1)}, u32[]{:S(2)}, u32[]{:S(2)}) collective-permute-start(bf16[2,2,96,768]{3,2,1,0:T(8,128)(2,1)} %get-tuple-element.224), channel_id=1, source_target_pairs={{0,1},{1,0},{2,3},{3,2},{4,5},{5,4},{6,7},{7,6},{8,9},{9,8},{10,11... | collective-permute-start | bytes 1769480 | tf_op jit(solution)/shard_map/ppermute | solution.py:25
  290.3 5.6 %collective-permute-start.39 = (bf16[2,2,96,768]{3,2,1,0:T(8,128)(2,1)}, bf16[2,2,96,768]{3,2,1,0:T(8,128)(2,1)S(1)}, u32[]{:S(2)}, u32[]{:S(2)}) collective-permute-start(bf16[2,2,96,768]{3,2,1,0:T(8,128)(2,1)} %get-tuple-element.226), channel_id=1, source_target_pairs={{0,1},{1,0},{2,3},{3,2},{4,5},{5,4},{6,7},{7,6},{8,9},{9,8},{10,11... | collective-permute-start | bytes 1769480 | tf_op jit(solution)/shard_map/ppermute | solution.py:25
  290.8 37.7 %all-to-all-start.4 = ((bf16[4,192,768]{2,1,0:T(8,128)(2,1)}), bf16[4,192,768]{2,1,0:T(8,128)(2,1)S(1)}, u32[]{:S(2)}, u32[]{:S(2)}) async-start(bf16[4,192,768]{2,1,0:T(8,128)(2,1)} %bitcast.39), calls=%async_computation.4 | async-start | bytes 2359296 | tf_op jit(solution)/shard_map/all_to_all | solution.py:479
  295.9 30.1 %collective-permute-start.42 = (bf16[4,2,96,768]{3,2,1,0:T(8,128)(2,1)}, bf16[4,2,96,768]{3,2,1,0:T(8,128)(2,1)S(1)}, u32[]{:S(2)}, u32[]{:S(2)}) collective-permute-start(bf16[4,2,96,768]{3,2,1,0:T(8,128)(2,1)} %get-tuple-element.232), channel_id=1, source_target_pairs={{0,1},{1,0},{2,3},{3,2},{4,5},{5,4},{6,7},{7,6},{8,9},{9,8},{10,11... | collective-permute-start | bytes 3538952 | tf_op jit(solution)/shard_map/ppermute | solution.py:25
  296.3 30.5 %collective-permute-start.43 = (bf16[4,2,96,768]{3,2,1,0:T(8,128)(2,1)S(1)}, bf16[4,2,96,768]{3,2,1,0:T(8,128)(2,1)S(1)}, u32[]{:S(2)}, u32[]{:S(2)}) collective-permute-start(bf16[4,2,96,768]{3,2,1,0:T(8,128)(2,1)S(1)} %fusion), channel_id=1, source_target_pairs={{0,4},{4,0},{8,12},{12,8},{16,20},{20,16},{24,28},{28,24},{1,5},{5... | collective-permute-start | bytes 3538952 | tf_op jit(solution)/shard_map/ppermute | solution.py:25
  297.2 28.8 %collective-permute-start.40 = (bf16[384,768]{1,0:T(8,128)(2,1)S(1)}, bf16[384,768]{1,0:T(8,128)(2,1)S(1)}, u32[]{:S(2)}, u32[]{:S(2)}) collective-permute-start(bf16[384,768]{1,0:T(8,128)(2,1)S(1)} %pad_maximum_fusion.5), channel_id=1, source_target_pairs={{0,2},{1,3},{2,0},{3,1},{4,6},{5,7},{6,4},{7,5},{8,10},{9,11},{10,... | collective-permute-start | bytes 1769480 | tf_op jit(solution)/shard_map/ppermute | solution.py:25
  298.6 1.2 collective-permute-start.44
  298.7 27.3 %collective-permute-start.41 = (bf16[8,32,768]{2,1,0:T(8,128)(2,1)S(1)}, bf16[8,32,768]{2,1,0:T(8,128)(2,1)S(1)}, u32[]{:S(2)}, u32[]{:S(2)}) collective-permute-start(bf16[8,32,768]{2,1,0:T(8,128)(2,1)S(1)} %copy-done.5), channel_id=1, source_target_pairs={{0,2},{1,3},{2,0},{3,1},{4,6},{5,7},{6,4},{7,5},{8,10},{9,11},{10,... | collective-permute-start | bytes 1179656 | tf_op jit(solution)/shard_map/ppermute | solution.py:25
  299.8 25.4 %collective-permute-start.45 = (bf16[16,768]{1,0:T(8,128)(2,1)S(1)}, bf16[16,768]{1,0:T(8,128)(2,1)S(1)}, u32[]{:S(2)}, u32[]{:S(2)}) collective-permute-start(bf16[16,768]{1,0:T(8,128)(2,1)S(1)} %add_convert_fusion.5), channel_id=1, source_target_pairs={{0,4},{4,0},{8,12},{12,8},{16,20},{20,16},{24,28},{28,24},{1,5},{5... | collective-permute-start | bytes 73736 | tf_op jit(solution)/shard_map/ppermute | solution.py:25
  325.2 31.9 %collective-permute-start.49 = (bf16[8,64,768]{2,1,0:T(8,128)(2,1)}, bf16[8,64,768]{2,1,0:T(8,128)(2,1)}, u32[]{:S(2)}, u32[]{:S(2)}) collective-permute-start(bf16[8,64,768]{2,1,0:T(8,128)(2,1)} %get-tuple-element.243), channel_id=1, source_target_pairs={{0,3},{1,2},{2,1},{3,0},{4,7},{5,6},{6,5},{7,4},{8,11},{9,10},{10,... | collective-permute-start | bytes 2359304 | tf_op jit(solution)/shard_map/ppermute | solution.py:25
  325.9 35.3 %copy-start.7 = (bf16[8,32,768]{2,1,0:T(8,128)(2,1)}, bf16[8,32,768]{2,1,0:T(8,128)(2,1)S(1)}, u32[]{:S(2)}) copy-start(bf16[8,32,768]{2,1,0:T(8,128)(2,1)S(1)} %collective-permute-done.41.refs_2_) | copy-start | bytes 1179652
  329.4 22.1 %collective-permute-start.52 = (bf16[192,768]{1,0:T(8,128)(2,1)}, bf16[192,768]{1,0:T(8,128)(2,1)}, u32[]{:S(2)}, u32[]{:S(2)}) collective-permute-start(bf16[192,768]{1,0:T(8,128)(2,1)} %reduce_sum.44), channel_id=1, source_target_pairs={{0,2},{1,3},{2,0},{3,1},{4,6},{5,7},{6,4},{7,5},{8,10},{9,11},{10,... | collective-permute-start | bytes 884744 | tf_op jit(solution)/shard_map/ppermute | solution.py:25
  330.1 31.2 %collective-permute-start.47 = (bf16[8,32,768]{2,1,0:T(8,128)(2,1)S(1)}, bf16[8,32,768]{2,1,0:T(8,128)(2,1)S(1)}, u32[]{:S(2)}, u32[]{:S(2)}) collective-permute-start(bf16[8,32,768]{2,1,0:T(8,128)(2,1)S(1)} %copy-done.6), channel_id=1, source_target_pairs={{0,2},{1,3},{2,0},{3,1},{4,6},{5,7},{6,4},{7,5},{8,10},{9,11},{10,... | collective-permute-start | bytes 1179656 | tf_op jit(solution)/shard_map/ppermute | solution.py:25
  351.6 10.0 %collective-permute-start.53 = (bf16[192,768]{1,0:T(8,128)(2,1)}, bf16[192,768]{1,0:T(8,128)(2,1)}, u32[]{:S(2)}, u32[]{:S(2)}) collective-permute-start(bf16[192,768]{1,0:T(8,128)(2,1)} %reduce_sum.44), channel_id=1, source_target_pairs={{0,1},{1,0},{2,3},{3,2},{4,5},{5,4},{6,7},{7,6},{8,9},{9,8},{10,11... | collective-permute-start | bytes 884744 | tf_op jit(solution)/shard_map/ppermute | solution.py:25
  351.7 10.3 %collective-permute-start.54 = (bf16[192,768]{1,0:T(8,128)(2,1)}, bf16[192,768]{1,0:T(8,128)(2,1)}, u32[]{:S(2)}, u32[]{:S(2)}) collective-permute-start(bf16[192,768]{1,0:T(8,128)(2,1)} %collective-permute-done.52), channel_id=1, source_target_pairs={{0,1},{1,0},{2,3},{3,2},{4,5},{5,4},{6,7},{7,6},{8,9},{9,8},{10,11... | collective-permute-start | bytes 884744 | tf_op jit(solution)/shard_map/ppermute | solution.py:25
  352.1 36.1 %all-to-all-start.3 = ((bf16[4,208,768]{2,1,0:T(8,128)(2,1)}), bf16[4,208,768]{2,1,0:T(8,128)(2,1)S(1)}, u32[]{:S(2)}, u32[]{:S(2)}) async-start(bf16[4,208,768]{2,1,0:T(8,128)(2,1)} %pad_maximum_fusion.1), calls=%async_computation.3 | async-start | bytes 2555904 | tf_op jit(solution)/shard_map/all_to_all | solution.py:479
  357.2 7.2 %collective-permute-start.50 = (bf16[384,768]{1,0:T(8,128)(2,1)S(1)}, bf16[384,768]{1,0:T(8,128)(2,1)S(1)}, u32[]{:S(2)}, u32[]{:S(2)}) collective-permute-start(bf16[384,768]{1,0:T(8,128)(2,1)S(1)} %pad_maximum_fusion.5), channel_id=1, source_target_pairs={{0,1},{1,0},{2,3},{3,2},{4,5},{5,4},{6,7},{7,6},{8,9},{9,8},{10,11... | collective-permute-start | bytes 1769480 | tf_op jit(solution)/shard_map/ppermute | solution.py:25
  357.2 8.0 %collective-permute-start.51 = (bf16[384,768]{1,0:T(8,128)(2,1)}, bf16[384,768]{1,0:T(8,128)(2,1)}, u32[]{:S(2)}, u32[]{:S(2)}) collective-permute-start(bf16[384,768]{1,0:T(8,128)(2,1)} %copy-done.24), channel_id=1, source_target_pairs={{0,1},{1,0},{2,3},{3,2},{4,5},{5,4},{6,7},{7,6},{8,9},{9,8},{10,11... | collective-permute-start | bytes 1769480 | tf_op jit(solution)/shard_map/ppermute | solution.py:25
  361.3 8.6 %collective-permute-start.46 = (bf16[2,8,32,768]{3,2,1,0:T(8,128)(2,1)S(1)}, bf16[2,8,32,768]{3,2,1,0:T(8,128)(2,1)S(1)}, u32[]{:S(2)}, u32[]{:S(2)}) collective-permute-start(bf16[2,8,32,768]{3,2,1,0:T(8,128)(2,1)S(1)} %pad_maximum_fusion.8), channel_id=1, source_target_pairs={{0,1},{1,0},{2,3},{3,2},{4,5},{5,4},{6,7},{7,6},{8,9},{9,8},{10,11... | collective-permute-start | bytes 2359304 | tf_op jit(solution)/shard_map/ppermute | solution.py:25
  361.5 8.4 %collective-permute-start.48 = (bf16[2,8,32,768]{3,2,1,0:T(8,128)(2,1)S(1)}, bf16[2,8,32,768]{3,2,1,0:T(8,128)(2,1)S(1)}, u32[]{:S(2)}, u32[]{:S(2)}) collective-permute-start(bf16[2,8,32,768]{3,2,1,0:T(8,128)(2,1)S(1)} %pad_maximum_fusion.9), channel_id=1, source_target_pairs={{0,1},{1,0},{2,3},{3,2},{4,5},{5,4},{6,7},{7,6},{8,9},{9,8},{10,11... | collective-permute-start | bytes 2359304 | tf_op jit(solution)/shard_map/ppermute | solution.py:25
  388.4 8.6 %collective-permute-start.55 = (bf16[208,768]{1,0:T(8,128)(2,1)S(1)}, bf16[208,768]{1,0:T(8,128)(2,1)S(1)}, u32[]{:S(2)}, u32[]{:S(2)}) collective-permute-start(bf16[208,768]{1,0:T(8,128)(2,1)S(1)} %reduce_sum.45), channel_id=1, source_target_pairs={{0,2},{1,3},{2,0},{3,1},{4,6},{5,7},{6,4},{7,5},{8,10},{9,11},{10,... | collective-permute-start | bytes 958472 | tf_op jit(solution)/shard_map/ppermute | solution.py:25
  397.1 2.1 collective-permute-start.56
  397.2 2.0 collective-permute-start.57
  (49 other events, 284.9 us)
where the time goes:
time: 409 us; the launch traced here: 401 us
  waiting for transfers between devices  160 us (39%)
  Pallas kernels  112 us (27%)
  starting transfers between devices  79.9 us (20%)
  other arithmetic  30.2 us (7%)
  local copies, waits for them, and re-layouts  17.6 us (4%)
    ppermute x58, waiting for transfers between devices, swap(): return lax.ppermute(value, axis, [(i, i ^ distance) for i in range(size)])  133 us
    pallas_call x10, Pallas kernels, run(): pl.pallas_call(body, grid=grid, in_specs=[spec for spec, _ in flat_in], o...  112 us
    ppermute x58, starting transfers between devices, swap(): return lax.ppermute(value, axis, [(i, i ^ distance) for i in range(size)])  51.9 us
    all_to_all x4, waiting for transfers between devices, over_slow(): lax.all_to_all(value, 'fsdp', 0, 0, axis_index_groups=groups, tiled=True)  26.8 us
    all_to_all x4, starting transfers between devices, over_slow(): lax.all_to_all(value, 'fsdp', 0, 0, axis_index_groups=groups, tiled=True)  23.6 us
    unnamed x100, local copies, waits for them, and re-layouts  9.26 us
  transfers between devices with their start and end apart: 63, of which 22 were waited for; matrix products, arithmetic and copies ran while one was open for 8% of the time, Pallas kernels for 28%

commit v1 on v0

--- a/solution.py
+++ b/solution.py
@@ -524,10 +524,12 @@
         self.came = [swap(part, "fsdp", b + 1) for b, part in enumerate(self.out)]
         if self.vectors is not None:
             low = self.vectors.astype(BF)
-            came = [swap(low, "fsdp", b) for b in range(1, self.fast)]
-            self.vectors = sum(part.astype(F32) for part in [low, *came])
+            self.vectors = [low] + [swap(low, "fsdp", b) for b in range(1, self.fast)]
 
     def add_fast(self, *others):
+        if self.vectors is not None:
+            self.vectors, self.came = lax.optimization_barrier((self.vectors, self.came))
+            self.vectors = sum(part.astype(F32) for part in self.vectors)
         total = after(self.near, *others).astype(F32) + self.sent[0].astype(F32)
         for part in self.came:
             total = total + part.astype(F32)
@@ -823,7 +825,8 @@
     cross_scatter = scatter(grads, in_total, *mem_pieces[1:3])
     cross_sum = cross_scatter.add_cores()
     cross_scatter.send_fast()
-    gx1 = after(gx1, *cross_sum)
+    in_final = in_scatter.add_slow()
+    gx1 = after(gx1, in_final, *cross_sum)
     suffix_part, vecs_self, *grads = run(
         functools.partial(self_backward, group),
         [(SMEM, where), (ANY, suffix), (VMEM, vec), (VMEM, gx1), (VMEM, a1)]
@@ -833,12 +836,11 @@
         [square, own_rows, square, scratch(rows, 3 * width), scratch(*wide)],
         1 + blocks,
     )
-    in_final = in_scatter.add_slow(suffix_part)
-    cross_total = cross_scatter.add_fast(suffix_part)
-    cross_scatter.send_slow()
-    self_scatter = scatter(grads, in_final, cross_total, vectors=vecs_self)
+    self_scatter = scatter(grads, *mem_pieces[3:4], vectors=vecs_self)
     self_sum = self_scatter.add_cores()
     self_scatter.send_fast()
+    cross_scatter.add_fast(*self_sum)
+    cross_scatter.send_slow()
     dense_sum = after(jnp.concatenate([out_final, in_final]), *self_sum)
     dense_sum = Replicas(dense_sum, 2 * part, across)
     y_rows = spread_across(after(y, *self_sum), mem)
@@ -857,7 +859,13 @@
         [scratch(mem, examples, slots, width)],
         2 * mem,
     )
-    cross_sum.swap_cores()
+    (out_low, in_low, out_high, in_high), _ = dense_sum.combine(c)
+    grad_in = jnp.concatenate([in_low[:part], in_low[part:], in_high[:part], in_high[part:]], axis=1)
+    grad_out = jnp.concatenate([out_low, out_high])
+    done = [*cross_sum.halves, *suffix_rows, grad_in, grad_out, y_far, memory_grad]
+    self_final = Replicas(self_scatter.add_slow(*done), part, across)
+    cross_sum.swap_cores(self_final.halves[0])
+    suffix_rows = [after(value, self_final.halves[0]) for value in suffix_rows]
     suffix_far = swap(jnp.stack(suffix_rows), "mem", 1)
     blocks = [([(ANY, x) for x in y_rows], (ANY, y_far))]
     blocks += [([(ANY, x) for x in suffix_rows], (ANY, suffix_far))]
@@ -868,13 +876,8 @@
         [scratch(2, mem, examples, length, width)],
         4 * mem,
     )
-    (out_low, in_low, out_high, in_high), _ = dense_sum.combine(c)
-    grad_in = jnp.concatenate([in_low[:part], in_low[part:], in_high[:part], in_high[part:]], axis=1)
-    grad_out = jnp.concatenate([out_low, out_high])
     grad_cross, _ = cross_sum.combine(c)
-    done = [grad_in, grad_out, *grad_cross, block_output, memory_grad]
-    self_final = Replicas(self_scatter.add_slow(*done), part, across)
-    self_final.swap_cores()
+    self_final.swap_cores(block_output)
     grad_self, vectors = self_final.combine(c)
 
     def vector(i):

time: 409 us -> 390 us (0.954); the launches traced: 401 us -> 387 us
  waiting for transfers between devices: 160 us -> 128 us
  Pallas kernels: 112 us -> 123 us
  other arithmetic: 30.2 us -> 37.6 us
    ppermute x58, waiting for transfers between devices: 133 us -> 109 us  [swap(): return lax.ppermute(value, axis, [(i, i ^ distance) for i in range(size)])]
    pallas_call x10, Pallas kernels: 112 us -> 123 us  [run(): pl.pallas_call(body, grid=grid, in_specs=[spec for spec, _ in flat_in], o...]
    all_to_all x4, waiting for transfers between devices: 26.8 us -> 18.8 us  [over_slow(): lax.all_to_all(value, 'fsdp', 0, 0, axis_index_groups=groups, tiled=True)]
    unnamed x100 -> x80, local copies, waits for them, and re-layouts: 9.26 us -> 7.55 us
  transfers between devices with their start and end apart: 63 -> 63, of which waited for: 22 -> 23; matrix products, arithmetic and copies ran while one was open for 8% -> 11% of each run, Pallas kernels for 28% -> 32%
where the time goes in v1:
time: 390 us; the launch traced here: 387 us
  waiting for transfers between devices  128 us (33%)
  Pallas kernels  123 us (32%)
  starting transfers between devices  79.5 us (20%)
  other arithmetic  37.6 us (10%)
  local copies, waits for them, and re-layouts  17.4 us (4%)
    pallas_call x10, Pallas kernels, run(): pl.pallas_call(body, grid=grid, in_specs=[spec for spec, _ in flat_in], o...  123 us
    ppermute x58, waiting for transfers between devices, swap(): return lax.ppermute(value, axis, [(i, i ^ distance) for i in range(size)])  109 us
    ppermute x58, starting transfers between devices, swap(): return lax.ppermute(value, axis, [(i, i ^ distance) for i in range(size)])  51.4 us
    all_to_all x4, starting transfers between devices, over_slow(): lax.all_to_all(value, 'fsdp', 0, 0, axis_index_groups=groups, tiled=True)  23.7 us
    all_to_all x4, waiting for transfers between devices, over_slow(): lax.all_to_all(value, 'fsdp', 0, 0, axis_index_groups=groups, tiled=True)  18.8 us
    convert_element_type x4, other arithmetic, add_fast(): self.total = total.astype(BF).reshape(self.slow, -1, total.shape[-1])  8.13 us
  transfers between devices with their start and end apart: 63, of which 23 were waited for; matrix products, arithmetic and copies ran while one was open for 11% of the time, Pallas kernels for 32%

profile of v1, /device:TPU:0, one launch (start us, length us, event | category | flops | bytes accessed | tf_op | source)
XLA Modules:
  0.0 387.2 jit_solution(2758412742487824005)
XLA Ops:
  0.8 4.4 %all-to-all-start = ((bf16[4,8,64,768]{3,2,1,0:T(8,128)(2,1)}), bf16[4,8,64,768]{3,2,1,0:T(8,128)(2,1)S(1)}, u32[]{:S(2)}, u32[]{:S(2)}) async-start(bf16[4,8,64,768]{3,2,1,0:T(8,128)(2,1)} %bitcast.73), calls=%async_computation | async-start | bytes 6291456 | tf_op jit(solution)/shard_map/all_to_all | solution.py:676
  6.4 2.6 collective-permute-start
  9.0 2.6 collective-permute-start.1
  11.6 12.0 %collective-permute-done = bf16[208,768]{1,0:T(8,128)(2,1)S(1)} collective-permute-done((bf16[208,768]{1,0:T(8,128)(2,1)S(1)}, bf16[208,768]{1,0:T(8,128)(2,1)S(1)}, u32[]{:S(2)}, u32[]{:S(2)}) %collective-permute-start) | collective-permute-done | bytes 319520 | tf_op jit(solution)/shard_map/ppermute | solution.py:25
  23.5 10.5 %collective-permute-done.1 = bf16[208,768]{1,0:T(8,128)(2,1)S(1)} collective-permute-done((bf16[208,768]{1,0:T(8,128)(2,1)S(1)}, bf16[208,768]{1,0:T(8,128)(2,1)S(1)}, u32[]{:S(2)}, u32[]{:S(2)}) %collective-permute-start.1) | collective-permute-done | bytes 319520 | tf_op jit(solution)/shard_map/ppermute | solution.py:25
  34.0 1.2 pad_maximum_fusion.refs_2_.refs_12_
  35.3 1.6 collective-permute-start.3
  37.1 6.7 %collective-permute-start.4 = (bf16[192,768]{1,0:T(8,128)(2,1)S(1)}, bf16[192,768]{1,0:T(8,128)(2,1)S(1)}, u32[]{:S(2)}, u32[]{:S(2)}) collective-permute-start(bf16[192,768]{1,0:T(8,128)(2,1)S(1)} %get-tuple-element.149), channel_id=1, source_target_pairs={{0,8},{4,12},{8,0},{12,4},{16,24},{20,28},{24,16},{28,20},{1,9},{5... | collective-permute-start | bytes 884744 | tf_op jit(solution)/shard_map/ppermute | solution.py:25
  44.9 1.4 collective-permute-start.6
  46.3 8.9 %collective-permute-done.4 = bf16[192,768]{1,0:T(8,128)(2,1)S(1)} collective-permute-done((bf16[192,768]{1,0:T(8,128)(2,1)S(1)}, bf16[192,768]{1,0:T(8,128)(2,1)S(1)}, u32[]{:S(2)}, u32[]{:S(2)}) %collective-permute-start.4) | collective-permute-done | bytes 294944 | tf_op jit(solution)/shard_map/ppermute | solution.py:25
  55.2 12.1 %collective-permute-done.5 = bf16[192,768]{1,0:T(8,128)(2,1)S(1)} collective-permute-done((bf16[192,768]{1,0:T(8,128)(2,1)S(1)}, bf16[192,768]{1,0:T(8,128)(2,1)S(1)}, u32[]{:S(2)}, u32[]{:S(2)}) %collective-permute-start.5) | collective-permute-done | bytes 294944 | tf_op jit(solution)/shard_map/ppermute | solution.py:25
  68.8 3.3 pad_maximum_fusion.2.refs_5_.refs_7_
  73.0 4.3 %collective-permute-start.10 = (bf16[192,768]{1,0:T(8,128)(2,1)S(1)}, bf16[192,768]{1,0:T(8,128)(2,1)}, u32[]{:S(2)}, u32[]{:S(2)}) collective-permute-start(bf16[192,768]{1,0:T(8,128)(2,1)S(1)} %get-tuple-element.158), channel_id=1, source_target_pairs={{0,8},{4,12},{8,0},{12,4},{16,24},{20,28},{24,16},{28,20},{1,9},{5... | collective-permute-start | bytes 884744 | tf_op jit(solution)/shard_map/ppermute | solution.py:25
  78.3 1.5 collective-permute-start.12
  80.4 7.6 %shard_map.373 = (f32[256,768]{1,0:T(8,128)}, bf16[256,768]{1,0:T(8,128)(2,1)}, bf16[256,2304]{1,0:T(8,128)(2,1)}, bf16[6,512,128]{2,1,0:T(8,128)(2,1)}, bf16[256,768]{1,0:T(8,128)(2,1)}, /*index=5*/f32[16,768]{1,0:T(8,128)}) custom-call(s32[4]{0:T(128)} %pad_add_fusion.1.refs_0_, bf16[32,32,768]{2,1,0:T(8,128)(2,1)} %refs_1_.5, ...), custom_call_target="tpu_custom_call" | custom-call | tf_op jit(solution)/shard_map/pallas_call | solution.py:458
  88.0 1.1 collective-permute-done.10
  89.2 11.7 %collective-permute-done.11 = bf16[192,768]{1,0:T(8,128)(2,1)} collective-permute-done((bf16[192,768]{1,0:T(8,128)(2,1)S(1)}, bf16[192,768]{1,0:T(8,128)(2,1)}, u32[]{:S(2)}, u32[]{:S(2)}) %collective-permute-start.11) | collective-permute-done | bytes 294944 | tf_op jit(solution)/shard_map/ppermute | solution.py:25
  100.9 1.4 pad_maximum_fusion.3.refs_5_
  103.2 5.0 %collective-permute-start.16 = (bf16[192,768]{1,0:T(8,128)(2,1)S(1)}, bf16[192,768]{1,0:T(8,128)(2,1)S(1)}, u32[]{:S(2)}, u32[]{:S(2)}) collective-permute-start(bf16[192,768]{1,0:T(8,128)(2,1)S(1)} %slice_select_fusion), channel_id=1, source_target_pairs={{0,8},{4,12},{8,0},{12,4},{16,24},{20,28},{24,16},{28,20},{1,9},{5... | collective-permute-start | bytes 884744 | tf_op jit(solution)/shard_map/ppermute | solution.py:25
  109.2 1.4 collective-permute-start.18
  111.7 16.8 %shard_map.374 = (f32[256,768]{1,0:T(8,128)}, bf16[256,768]{1,0:T(8,128)(2,1)}, bf16[256,768]{1,0:T(8,128)(2,1)}, bf16[8,256,1536]{2,1,0:T(8,128)(2,1)}, bf16[8,...) custom-call(s32[4]{0:T(128)} %pad_add_fusion.1.refs_0_, s32[32]{0:T(128)} %refs_1_.4, ...), custom_call_target="tpu_custom_call" | custom-call | tf_op jit(solution)/shard_map/pallas_call | solution.py:458
  128.5 3.1 collective-permute-done.17
  131.7 1.3 pad_maximum_fusion.4.refs_7_
  133.0 1.2 collective-permute-start.21
  136.2 1.2 gather_fusion
  140.0 13.6 %shard_map.375 = (bf16[256,768]{1,0:T(8,128)(2,1)}, bf16[256,3072]{1,0:T(8,128)(2,1)}, bf16[256,3072]{1,0:T(8,128)(2,1)}, bf16[4,2,96,768]{3,2,1,0:T(8,128)(2,1)...) custom-call(s32[4]{0:T(128)} %pad_add_fusion.1.refs_0_, ...), custom_call_target="tpu_custom_call" | custom-call | tf_op jit(solution)/shard_map/pallas_call | solution.py:458
  153.5 8.0 %collective-permute-done.21.refs_8_ = bf16[4,192,768]{2,1,0:T(8,128)(2,1)} collective-permute-done((bf16[4,192,768]{2,1,0:T(8,128)(2,1)}, bf16[4,192,768]{2,1,0:T(8,128)(2,1)}, u32[]{:S(2)}, u32[]{:S(2)}) %collective-permute-start.21) | collective-permute-done | bytes 1179680 | tf_op jit(solution)/shard_map/ppermute | solution.py:25
  162.5 2.9 collective-permute-done.22
  166.2 1.6 fusion.3
  167.8 1.3 collective-permute-start.29
  170.5 11.7 %shard_map.376 = (bf16[8,32,768]{2,1,0:T(8,128)(2,1)}, bf16[256,3072]{1,0:T(8,128)(2,1)}, f32[1,768]{1,0:T(1,128)}, f32[1,3072]{1,0:T(1,128)}, bf16[4,2,96,768]{...) custom-call(s32[4]{0:T(128)} %pad_add_fusion.1.refs_0_, ...), custom_call_target="tpu_custom_call" | custom-call | tf_op jit(solution)/shard_map/pallas_call | solution.py:458
  182.3 19.0 %shard_map.377 = (f32[256,768]{1,0:T(8,128)}, f32[2,768]{1,0:T(2,128)}) custom-call(s32[4]{0:T(128)} %pad_add_fusion.1.refs_0_, f32[256,768]{1,0:T(8,128)} %get-tuple-element.175.refs_1_, f32[16,768]{1,0:T(8,128)} %get-tuple-element.148.refs_3_.refs_2_, bf16[256,3072]{1,0:T(8,128)(2,1)} %get-tuple-element.179.refs_3_, bf16[32,32,768]{2,1,0:T(8,128)(2,1)} %refs_4_.3, ...), custom_call_target="tpu_custom_call" | custom-call | tf_op jit(solution)/shard_map/pallas_call | solution.py:458
  201.9 1.5 collective-permute-done.26
  205.5 1.5 add_convert_fusion.3
  207.0 8.1 %all-to-all-start.2 = ((bf16[4,192,768]{2,1,0:T(8,128)(2,1)}), bf16[4,192,768]{2,1,0:T(8,128)(2,1)S(1)}, u32[]{:S(2)}, u32[]{:S(2)}) async-start(bf16[4,192,768]{2,1,0:T(8,128)(2,1)} %bitcast.35), calls=%async_computation.2 | async-start | bytes 2359296 | tf_op jit(solution)/shard_map/all_to_all | solution.py:479
  215.9 23.3 %shard_map.378 = (f32[256,768]{1,0:T(8,128)}, f32[2,768]{1,0:T(2,128)}, bf16[8,256,1536]{2,1,0:T(8,128)(2,1)}, bf16[256,768]{1,0:T(8,128)(2,1)}, bf16[8,64,768]{...) custom-call(s32[4]{0:T(128)} %pad_add_fusion.1.refs_0_, ...), custom_call_target="tpu_custom_call" | custom-call | tf_op jit(solution)/shard_map/pallas_call | solution.py:458
  239.5 1.4 collective-permute-start.33
  240.8 2.6 collective-permute-done.31
  243.4 1.5 add_convert_fusion.2
  244.9 5.1 %all-to-all-start.1 = ((bf16[4,192,768]{2,1,0:T(8,128)(2,1)}), bf16[4,192,768]{2,1,0:T(8,128)(2,1)S(1)}, u32[]{:S(2)}, u32[]{:S(2)}) async-start(bf16[4,192,768]{2,1,0:T(8,128)(2,1)} %bitcast.36), calls=%async_computation.1 | async-start | bytes 2359296 | tf_op jit(solution)/shard_map/all_to_all | solution.py:479
  250.9 12.8 %shard_map.379 = (bf16[4,2,96,768]{3,2,1,0:T(8,128)(2,1)}, bf16[1,4,2,96,768]{4,3,2,1,0:T(8,128)(2,1)}, bf16[4,2,96,768]{3,2,1,0:T(8,128)(2,1)}, bf16[2,2,96,768]{3,2,1,0:T(8,128)(2,1)}, bf16[2,2,96,768]{3,2,1,0:T(8,128)(2,1)}) custom-call(s32[4]{0:T(128)} %pad_add_fusion.1.refs_0_, f32[256,768]{1,0:T(8,128)} %get-tuple-element.199.refs_3_.refs_1_, ...), custom_call_target="tpu_custom_call" | custom-call | tf_op jit(solution)/shard_map/pallas_call | solution.py:458
  266.8 1.6 fusion.1
  269.3 9.2 %all-to-all-done.1 = bf16[4,192,768]{2,1,0:T(8,128)(2,1)S(1)} async-done(((bf16[4,192,768]{2,1,0:T(8,128)(2,1)}), bf16[4,192,768]{2,1,0:T(8,128)(2,1)S(1)}, u32[]{:S(2)}, u32[]{:S(2)}) %all-to-all-start.1) | async-done | bytes 1179680 | tf_op jit(solution)/shard_map/all_to_all | solution.py:479
  279.3 11.7 %shard_map.380 = (bf16[8,32,768]{2,1,0:T(8,128)(2,1)}, bf16[16,768]{1,0:T(8,128)(2,1)}, bf16[4,2,96,768]{3,2,1,0:T(8,128)(2,1)}, bf16[1,4,2,96,768]{4,3,2,1,0:T(...) custom-call(s32[4]{0:T(128)} %pad_add_fusion.1.refs_0_, ...), custom_call_target="tpu_custom_call" | custom-call | tf_op jit(solution)/shard_map/pallas_call | solution.py:458
  291.6 1.7 collective-permute-done.37
  294.1 1.7 fusion
  296.7 3.1 add_convert_fusion
  299.8 5.4 %all-to-all-start.4 = ((bf16[4,192,768]{2,1,0:T(8,128)(2,1)}), bf16[4,192,768]{2,1,0:T(8,128)(2,1)S(1)}, u32[]{:S(2)}, u32[]{:S(2)}) async-start(bf16[4,192,768]{2,1,0:T(8,128)(2,1)} %bitcast.42), calls=%async_computation.4 | async-start | bytes 2359296 | tf_op jit(solution)/shard_map/all_to_all | solution.py:479
  306.4 1.4 collective-permute-start.39
  308.5 1.2 collective-permute-done.42
  310.6 20.0 %collective-permute-done.40.refs_2_ = bf16[8,32,768]{2,1,0:T(8,128)(2,1)S(1)} collective-permute-done((bf16[8,32,768]{2,1,0:T(8,128)(2,1)S(1)}, bf16[8,32,768]{2,1,0:T(8,128)(2,1)S(1)}, u32[]{:S(2)}, u32[]{:S(2)}) %collective-permute-start.40) | collective-permute-done | bytes 393248 | tf_op jit(solution)/shard_map/ppermute | solution.py:25
  331.4 2.1 add_convert_fusion.1
  335.2 5.1 %all-to-all-start.3 = ((bf16[4,208,768]{2,1,0:T(8,128)(2,1)}), bf16[4,208,768]{2,1,0:T(8,128)(2,1)S(1)}, u32[]{:S(2)}, u32[]{:S(2)}) async-start(bf16[4,208,768]{2,1,0:T(8,128)(2,1)} %pad_maximum_fusion.1), calls=%async_computation.3 | async-start | bytes 2555904 | tf_op jit(solution)/shard_map/all_to_all | solution.py:479
  340.3 1.4 collective-permute-start.49
  341.7 1.9 pad_maximum_fusion.8
  343.6 3.5 shard_map.381
  347.2 1.7 fusion.5
  352.7 2.2 pad_maximum_fusion.6
  354.8 6.6 %collective-permute-done.48 = bf16[192,768]{1,0:T(8,128)(2,1)S(1)} collective-permute-done((bf16[192,768]{1,0:T(8,128)(2,1)S(1)}, bf16[192,768]{1,0:T(8,128)(2,1)S(1)}, u32[]{:S(2)}, u32[]{:S(2)}) %collective-permute-start.48) | collective-permute-done | bytes 294944 | tf_op jit(solution)/shard_map/ppermute | solution.py:25
  361.4 9.7 %all-to-all-done.3 = bf16[4,208,768]{2,1,0:T(8,128)(2,1)S(1)} async-done(((bf16[4,208,768]{2,1,0:T(8,128)(2,1)}), bf16[4,208,768]{2,1,0:T(8,128)(2,1)S(1)}, u32[]{:S(2)}, u32[]{:S(2)}) %all-to-all-start.3) | async-done | bytes 1277984 | tf_op jit(solution)/shard_map/all_to_all | solution.py:479
  373.2 1.4 collective-permute-start.53
  374.6 1.2 fusion.8
  378.4 3.4 shard_map.382
  381.8 1.3 collective-permute-done.53
  (213 shorter events, 46.8 us)
Async XLA Ops:
  0.8 67.9 %all-to-all-start = ((bf16[4,8,64,768]{3,2,1,0:T(8,128)(2,1)}), bf16[4,8,64,768]{3,2,1,0:T(8,128)(2,1)S(1)}, u32[]{:S(2)}, u32[]{:S(2)}) async-start(bf16[4,8,64,768]{3,2,1,0:T(8,128)(2,1)} %bitcast.73), calls=%async_computation | async-start | bytes 6291456 | tf_op jit(solution)/shard_map/all_to_all | solution.py:676
  6.4 17.2 %collective-permute-start = (bf16[208,768]{1,0:T(8,128)(2,1)S(1)}, bf16[208,768]{1,0:T(8,128)(2,1)S(1)}, u32[]{:S(2)}, u32[]{:S(2)}) collective-permute-start(bf16[208,768]{1,0:T(8,128)(2,1)S(1)} %pad_maximum_fusion.10), channel_id=1, source_target_pairs={{0,8},{4,12},{8,0},{12,4},{16,24},{20,28},{24,16},{28,20},{1,9},{5... | collective-permute-start | bytes 958472 | tf_op jit(solution)/shard_map/ppermute | solution.py:25
  9.0 25.0 %collective-permute-start.1 = (bf16[208,768]{1,0:T(8,128)(2,1)S(1)}, bf16[208,768]{1,0:T(8,128)(2,1)S(1)}, u32[]{:S(2)}, u32[]{:S(2)}) collective-permute-start(bf16[208,768]{1,0:T(8,128)(2,1)S(1)} %pad_maximum_fusion.10), channel_id=1, source_target_pairs={{0,16},{4,20},{8,24},{12,28},{16,0},{20,4},{24,8},{28,12},{1,17},{... | collective-permute-start | bytes 958472 | tf_op jit(solution)/shard_map/ppermute | solution.py:25
  11.6 22.4 %collective-permute-start.2 = (bf16[208,768]{1,0:T(8,128)(2,1)S(1)}, bf16[208,768]{1,0:T(8,128)(2,1)S(1)}, u32[]{:S(2)}, u32[]{:S(2)}) collective-permute-start(bf16[208,768]{1,0:T(8,128)(2,1)S(1)} %pad_maximum_fusion.10), channel_id=1, source_target_pairs={{0,24},{4,28},{8,16},{12,20},{16,8},{20,12},{24,0},{28,4},{1,25},{... | collective-permute-start | bytes 958472 | tf_op jit(solution)/shard_map/ppermute | solution.py:25
  35.3 33.4 %collective-permute-start.3 = (bf16[4,208,768]{2,1,0:T(8,128)(2,1)}, bf16[4,208,768]{2,1,0:T(8,128)(2,1)}, u32[]{:S(2)}, u32[]{:S(2)}) collective-permute-start(bf16[4,208,768]{2,1,0:T(8,128)(2,1)} %pad_maximum_fusion.refs_2_.refs_12_), channel_id=1, source_target_pairs={{0,4},{4,0},{8,12},{12,8},{16,20},{20,16},{24,28},{28,24},{1,5},{5... | collective-permute-start | bytes 3833864 | tf_op jit(solution)/shard_map/ppermute | solution.py:25
  37.1 30.2 %copy-start.9 = (bf16[192,768]{1,0:T(8,128)(2,1)}, bf16[192,768]{1,0:T(8,128)(2,1)S(1)}, u32[]{:S(2)}) copy-start(bf16[192,768]{1,0:T(8,128)(2,1)S(1)} %get-tuple-element.149) | copy-start | bytes 884740
  37.1 18.1 %collective-permute-start.4 = (bf16[192,768]{1,0:T(8,128)(2,1)S(1)}, bf16[192,768]{1,0:T(8,128)(2,1)S(1)}, u32[]{:S(2)}, u32[]{:S(2)}) collective-permute-start(bf16[192,768]{1,0:T(8,128)(2,1)S(1)} %get-tuple-element.149), channel_id=1, source_target_pairs={{0,8},{4,12},{8,0},{12,4},{16,24},{20,28},{24,16},{28,20},{1,9},{5... | collective-permute-start | bytes 884744 | tf_op jit(solution)/shard_map/ppermute | solution.py:25
  43.8 23.5 %collective-permute-start.5 = (bf16[192,768]{1,0:T(8,128)(2,1)S(1)}, bf16[192,768]{1,0:T(8,128)(2,1)S(1)}, u32[]{:S(2)}, u32[]{:S(2)}) collective-permute-start(bf16[192,768]{1,0:T(8,128)(2,1)S(1)} %get-tuple-element.149), channel_id=1, source_target_pairs={{0,16},{4,20},{8,24},{12,28},{16,0},{20,4},{24,8},{28,12},{1,17},{... | collective-permute-start | bytes 884744 | tf_op jit(solution)/shard_map/ppermute | solution.py:25
  44.9 22.4 %collective-permute-start.6 = (bf16[192,768]{1,0:T(8,128)(2,1)S(1)}, bf16[192,768]{1,0:T(8,128)(2,1)S(1)}, u32[]{:S(2)}, u32[]{:S(2)}) collective-permute-start(bf16[192,768]{1,0:T(8,128)(2,1)S(1)} %get-tuple-element.149), channel_id=1, source_target_pairs={{0,24},{4,28},{8,16},{12,20},{16,8},{20,12},{24,0},{28,4},{1,25},{... | collective-permute-start | bytes 884744 | tf_op jit(solution)/shard_map/ppermute | solution.py:25
  46.3 32.0 %collective-permute-start.7 = (bf16[4,208,768]{2,1,0:T(8,128)(2,1)}, bf16[4,208,768]{2,1,0:T(8,128)(2,1)}, u32[]{:S(2)}, u32[]{:S(2)}) collective-permute-start(bf16[4,208,768]{2,1,0:T(8,128)(2,1)} %pad_maximum_fusion.refs_2_.refs_12_), channel_id=1, source_target_pairs={{0,1},{1,0},{2,3},{3,2},{4,5},{5,4},{6,7},{7,6},{8,9},{9,8},{10,11... | collective-permute-start | bytes 3833864 | tf_op jit(solution)/shard_map/ppermute | solution.py:25
  68.7 11.1 %collective-permute-start.8 = (bf16[4,208,768]{2,1,0:T(8,128)(2,1)}, bf16[4,208,768]{2,1,0:T(8,128)(2,1)}, u32[]{:S(2)}, u32[]{:S(2)}) collective-permute-start(bf16[4,208,768]{2,1,0:T(8,128)(2,1)} %collective-permute-done.3.refs_3_.refs_13_), channel_id=1, source_target_pairs={{0,1},{1,0},{2,3},{3,2},{4,5},{5,4},{6,7},{7,6},{8,9},{9,8},{10,11... | collective-permute-start | bytes 3833864 | tf_op jit(solution)/shard_map/ppermute | solution.py:25
  72.1 28.8 %collective-permute-start.9 = (bf16[4,192,768]{2,1,0:T(8,128)(2,1)}, bf16[4,192,768]{2,1,0:T(8,128)(2,1)}, u32[]{:S(2)}, u32[]{:S(2)}) collective-permute-start(bf16[4,192,768]{2,1,0:T(8,128)(2,1)} %pad_maximum_fusion.2.refs_5_.refs_7_), channel_id=1, source_target_pairs={{0,4},{4,0},{8,12},{12,8},{16,20},{20,16},{24,28},{28,24},{1,5},{5... | collective-permute-start | bytes 3538952 | tf_op jit(solution)/shard_map/ppermute | solution.py:25
  73.0 16.1 %collective-permute-start.10 = (bf16[192,768]{1,0:T(8,128)(2,1)S(1)}, bf16[192,768]{1,0:T(8,128)(2,1)}, u32[]{:S(2)}, u32[]{:S(2)}) collective-permute-start(bf16[192,768]{1,0:T(8,128)(2,1)S(1)} %get-tuple-element.158), channel_id=1, source_target_pairs={{0,8},{4,12},{8,0},{12,4},{16,24},{20,28},{24,16},{28,20},{1,9},{5... | collective-permute-start | bytes 884744 | tf_op jit(solution)/shard_map/ppermute | solution.py:25
  77.3 23.6 %collective-permute-start.11 = (bf16[192,768]{1,0:T(8,128)(2,1)S(1)}, bf16[192,768]{1,0:T(8,128)(2,1)}, u32[]{:S(2)}, u32[]{:S(2)}) collective-permute-start(bf16[192,768]{1,0:T(8,128)(2,1)S(1)} %get-tuple-element.158), channel_id=1, source_target_pairs={{0,16},{4,20},{8,24},{12,28},{16,0},{20,4},{24,8},{28,12},{1,17},{... | collective-permute-start | bytes 884744 | tf_op jit(solution)/shard_map/ppermute | solution.py:25
  78.3 22.6 %collective-permute-start.12 = (bf16[192,768]{1,0:T(8,128)(2,1)S(1)}, bf16[192,768]{1,0:T(8,128)(2,1)}, u32[]{:S(2)}, u32[]{:S(2)}) collective-permute-start(bf16[192,768]{1,0:T(8,128)(2,1)S(1)} %get-tuple-element.158), channel_id=1, source_target_pairs={{0,24},{4,28},{8,16},{12,20},{16,8},{20,12},{24,0},{28,4},{1,25},{... | collective-permute-start | bytes 884744 | tf_op jit(solution)/shard_map/ppermute | solution.py:25
  79.8 29.5 %collective-permute-start.13 = (bf16[4,192,768]{2,1,0:T(8,128)(2,1)}, bf16[4,192,768]{2,1,0:T(8,128)(2,1)}, u32[]{:S(2)}, u32[]{:S(2)}) collective-permute-start(bf16[4,192,768]{2,1,0:T(8,128)(2,1)} %pad_maximum_fusion.2.refs_5_.refs_7_), channel_id=1, source_target_pairs={{0,1},{1,0},{2,3},{3,2},{4,5},{5,4},{6,7},{7,6},{8,9},{9,8},{10,11... | collective-permute-start | bytes 3538952 | tf_op jit(solution)/shard_map/ppermute | solution.py:25
  100.9 9.7 %collective-permute-start.14 = (bf16[4,192,768]{2,1,0:T(8,128)(2,1)}, bf16[4,192,768]{2,1,0:T(8,128)(2,1)S(1)}, u32[]{:S(2)}, u32[]{:S(2)}) collective-permute-start(bf16[4,192,768]{2,1,0:T(8,128)(2,1)} %collective-permute-done.9.refs_6_.refs_8_), channel_id=1, source_target_pairs={{0,1},{1,0},{2,3},{3,2},{4,5},{5,4},{6,7},{7,6},{8,9},{9,8},{10,11... | collective-permute-start | bytes 3538952 | tf_op jit(solution)/shard_map/ppermute | solution.py:25
  102.3 29.3 %collective-permute-start.15 = (bf16[4,192,768]{2,1,0:T(8,128)(2,1)S(1)}, bf16[4,192,768]{2,1,0:T(8,128)(2,1)S(1)}, u32[]{:S(2)}, u32[]{:S(2)}) collective-permute-start(bf16[4,192,768]{2,1,0:T(8,128)(2,1)S(1)} %pad_maximum_fusion.3.refs_5_), channel_id=1, source_target_pairs={{0,4},{4,0},{8,12},{12,8},{16,20},{20,16},{24,28},{28,24},{1,5},{5... | collective-permute-start | bytes 3538952 | tf_op jit(solution)/shard_map/ppermute | solution.py:25
  103.2 25.3 %collective-permute-start.16 = (bf16[192,768]{1,0:T(8,128)(2,1)S(1)}, bf16[192,768]{1,0:T(8,128)(2,1)S(1)}, u32[]{:S(2)}, u32[]{:S(2)}) collective-permute-start(bf16[192,768]{1,0:T(8,128)(2,1)S(1)} %slice_select_fusion), channel_id=1, source_target_pairs={{0,8},{4,12},{8,0},{12,4},{16,24},{20,28},{24,16},{28,20},{1,9},{5... | collective-permute-start | bytes 884744 | tf_op jit(solution)/shard_map/ppermute | solution.py:25
  108.1 23.4 %collective-permute-start.17 = (bf16[192,768]{1,0:T(8,128)(2,1)S(1)}, bf16[192,768]{1,0:T(8,128)(2,1)S(1)}, u32[]{:S(2)}, u32[]{:S(2)}) collective-permute-start(bf16[192,768]{1,0:T(8,128)(2,1)S(1)} %slice_select_fusion), channel_id=1, source_target_pairs={{0,16},{4,20},{8,24},{12,28},{16,0},{20,4},{24,8},{28,12},{1,17},{... | collective-permute-start | bytes 884744 | tf_op jit(solution)/shard_map/ppermute | solution.py:25
  109.2 22.3 %collective-permute-start.18 = (bf16[192,768]{1,0:T(8,128)(2,1)S(1)}, bf16[192,768]{1,0:T(8,128)(2,1)S(1)}, u32[]{:S(2)}, u32[]{:S(2)}) collective-permute-start(bf16[192,768]{1,0:T(8,128)(2,1)S(1)} %slice_select_fusion), channel_id=1, source_target_pairs={{0,24},{4,28},{8,16},{12,20},{16,8},{20,12},{24,0},{28,4},{1,25},{... | collective-permute-start | bytes 884744 | tf_op jit(solution)/shard_map/ppermute | solution.py:25
  110.6 28.3 %collective-permute-start.19 = (bf16[4,192,768]{2,1,0:T(8,128)(2,1)S(1)}, bf16[4,192,768]{2,1,0:T(8,128)(2,1)}, u32[]{:S(2)}, u32[]{:S(2)}) collective-permute-start(bf16[4,192,768]{2,1,0:T(8,128)(2,1)S(1)} %pad_maximum_fusion.3.refs_5_), channel_id=1, source_target_pairs={{0,1},{1,0},{2,3},{3,2},{4,5},{5,4},{6,7},{7,6},{8,9},{9,8},{10,11... | collective-permute-start | bytes 3538952 | tf_op jit(solution)/shard_map/ppermute | solution.py:25
  131.6 7.4 %collective-permute-start.20 = (bf16[4,192,768]{2,1,0:T(8,128)(2,1)S(1)}, bf16[4,192,768]{2,1,0:T(8,128)(2,1)S(1)}, u32[]{:S(2)}, u32[]{:S(2)}) collective-permute-start(bf16[4,192,768]{2,1,0:T(8,128)(2,1)S(1)} %collective-permute-done.15.refs_6_), channel_id=1, source_target_pairs={{0,1},{1,0},{2,3},{3,2},{4,5},{5,4},{6,7},{7,6},{8,9},{9,8},{10,11... | collective-permute-start | bytes 3538952 | tf_op jit(solution)/shard_map/ppermute | solution.py:25
  133.0 28.5 %collective-permute-start.21 = (bf16[4,192,768]{2,1,0:T(8,128)(2,1)}, bf16[4,192,768]{2,1,0:T(8,128)(2,1)}, u32[]{:S(2)}, u32[]{:S(2)}) collective-permute-start(bf16[4,192,768]{2,1,0:T(8,128)(2,1)} %pad_maximum_fusion.4.refs_7_), channel_id=1, source_target_pairs={{0,4},{4,0},{8,12},{12,8},{16,20},{20,16},{24,28},{28,24},{1,5},{5... | collective-permute-start | bytes 3538952 | tf_op jit(solution)/shard_map/ppermute | solution.py:25
  138.9 30.3 %collective-permute-start.24 = (bf16[4,192,768]{2,1,0:T(8,128)(2,1)}, bf16[4,192,768]{2,1,0:T(8,128)(2,1)S(1)}, u32[]{:S(2)}, u32[]{:S(2)}) collective-permute-start(bf16[4,192,768]{2,1,0:T(8,128)(2,1)} %pad_maximum_fusion.4.refs_7_), channel_id=1, source_target_pairs={{0,1},{1,0},{2,3},{3,2},{4,5},{5,4},{6,7},{7,6},{8,9},{9,8},{10,11... | collective-permute-start | bytes 3538952 | tf_op jit(solution)/shard_map/ppermute | solution.py:25
  161.5 7.6 %collective-permute-start.25 = (bf16[4,192,768]{2,1,0:T(8,128)(2,1)}, bf16[4,192,768]{2,1,0:T(8,128)(2,1)S(1)}, u32[]{:S(2)}, u32[]{:S(2)}) collective-permute-start(bf16[4,192,768]{2,1,0:T(8,128)(2,1)} %collective-permute-done.21.refs_8_), channel_id=1, source_target_pairs={{0,1},{1,0},{2,3},{3,2},{4,5},{5,4},{6,7},{7,6},{8,9},{9,8},{10,11... | collective-permute-start | bytes 3538952 | tf_op jit(solution)/shard_map/ppermute | solution.py:25
  161.5 3.9 %collective-permute-start.22 = (bf16[2,2,96,768]{3,2,1,0:T(8,128)(2,1)}, bf16[2,2,96,768]{3,2,1,0:T(8,128)(2,1)S(1)}, u32[]{:S(2)}, u32[]{:S(2)}) collective-permute-start(bf16[2,2,96,768]{3,2,1,0:T(8,128)(2,1)} %get-tuple-element.172), channel_id=1, source_target_pairs={{0,1},{1,0},{2,3},{3,2},{4,5},{5,4},{6,7},{7,6},{8,9},{9,8},{10,11... | collective-permute-start | bytes 1769480 | tf_op jit(solution)/shard_map/ppermute | solution.py:25
  162.0 4.2 %collective-permute-start.23 = (bf16[2,2,96,768]{3,2,1,0:T(8,128)(2,1)}, bf16[2,2,96,768]{3,2,1,0:T(8,128)(2,1)S(1)}, u32[]{:S(2)}, u32[]{:S(2)}) collective-permute-start(bf16[2,2,96,768]{3,2,1,0:T(8,128)(2,1)} %get-tuple-element.174), channel_id=1, source_target_pairs={{0,1},{1,0},{2,3},{3,2},{4,5},{5,4},{6,7},{7,6},{8,9},{9,8},{10,11... | collective-permute-start | bytes 1769480 | tf_op jit(solution)/shard_map/ppermute | solution.py:25
  162.0 42.5 %collective-permute-start.28 = (bf16[4,2,96,768]{3,2,1,0:T(8,128)(2,1)}, bf16[4,2,96,768]{3,2,1,0:T(8,128)(2,1)S(1)}, u32[]{:S(2)}, u32[]{:S(2)}) collective-permute-start(bf16[4,2,96,768]{3,2,1,0:T(8,128)(2,1)} %get-tuple-element.189), channel_id=1, source_target_pairs={{0,1},{1,0},{2,3},{3,2},{4,5},{5,4},{6,7},{7,6},{8,9},{9,8},{10,11... | collective-permute-start | bytes 3538952 | tf_op jit(solution)/shard_map/ppermute | solution.py:25
  167.8 36.7 %collective-permute-start.29 = (bf16[4,2,96,768]{3,2,1,0:T(8,128)(2,1)S(1)}, bf16[4,2,96,768]{3,2,1,0:T(8,128)(2,1)S(1)}, u32[]{:S(2)}, u32[]{:S(2)}) collective-permute-start(bf16[4,2,96,768]{3,2,1,0:T(8,128)(2,1)S(1)} %fusion.3), channel_id=1, source_target_pairs={{0,4},{4,0},{8,12},{12,8},{16,20},{20,16},{24,28},{28,24},{1,5},{5... | collective-permute-start | bytes 3538952 | tf_op jit(solution)/shard_map/ppermute | solution.py:25
  201.3 2.1 collective-permute-start.26
  201.4 2.8 collective-permute-start.27
  207.0 38.0 %all-to-all-start.2 = ((bf16[4,192,768]{2,1,0:T(8,128)(2,1)}), bf16[4,192,768]{2,1,0:T(8,128)(2,1)S(1)}, u32[]{:S(2)}, u32[]{:S(2)}) async-start(bf16[4,192,768]{2,1,0:T(8,128)(2,1)} %bitcast.35), calls=%async_computation.2 | async-start | bytes 2359296 | tf_op jit(solution)/shard_map/all_to_all | solution.py:479
  215.1 25.8 %collective-permute-start.30 = (bf16[4,2,96,768]{3,2,1,0:T(8,128)(2,1)}, bf16[4,2,96,768]{3,2,1,0:T(8,128)(2,1)S(1)}, u32[]{:S(2)}, u32[]{:S(2)}) collective-permute-start(bf16[4,2,96,768]{3,2,1,0:T(8,128)(2,1)} %get-tuple-element.197), channel_id=1, source_target_pairs={{0,1},{1,0},{2,3},{3,2},{4,5},{5,4},{6,7},{7,6},{8,9},{9,8},{10,11... | collective-permute-start | bytes 3538952 | tf_op jit(solution)/shard_map/ppermute | solution.py:25
  215.1 28.4 %collective-permute-start.31 = (bf16[4,2,96,768]{3,2,1,0:T(8,128)(2,1)S(1)}, bf16[4,2,96,768]{3,2,1,0:T(8,128)(2,1)S(1)}, u32[]{:S(2)}, u32[]{:S(2)}) collective-permute-start(bf16[4,2,96,768]{3,2,1,0:T(8,128)(2,1)S(1)} %fusion.2), channel_id=1, source_target_pairs={{0,4},{4,0},{8,12},{12,8},{16,20},{20,16},{24,28},{28,24},{1,5},{5... | collective-permute-start | bytes 3538952 | tf_op jit(solution)/shard_map/ppermute | solution.py:25
  239.2 24.5 %collective-permute-start.32 = (bf16[8,64,768]{2,1,0:T(8,128)(2,1)}, bf16[8,64,768]{2,1,0:T(8,128)(2,1)S(1)}, u32[]{:S(2)}, u32[]{:S(2)}) collective-permute-start(bf16[8,64,768]{2,1,0:T(8,128)(2,1)} %get-tuple-element.206), channel_id=1, source_target_pairs={{0,1},{1,0},{2,3},{3,2},{4,5},{5,4},{6,7},{7,6},{8,9},{9,8},{10,11... | collective-permute-start | bytes 2359304 | tf_op jit(solution)/shard_map/ppermute | solution.py:25
  239.5 24.2 %collective-permute-start.33 = (bf16[8,64,768]{2,1,0:T(8,128)(2,1)}, bf16[8,64,768]{2,1,0:T(8,128)(2,1)}, u32[]{:S(2)}, u32[]{:S(2)}) collective-permute-start(bf16[8,64,768]{2,1,0:T(8,128)(2,1)} %get-tuple-element.207), channel_id=1, source_target_pairs={{0,2},{1,3},{2,0},{3,1},{4,6},{5,7},{6,4},{7,5},{8,10},{9,11},{10,... | collective-permute-start | bytes 2359304 | tf_op jit(solution)/shard_map/ppermute | solution.py:25
  244.9 33.5 %all-to-all-start.1 = ((bf16[4,192,768]{2,1,0:T(8,128)(2,1)}), bf16[4,192,768]{2,1,0:T(8,128)(2,1)S(1)}, u32[]{:S(2)}, u32[]{:S(2)}) async-start(bf16[4,192,768]{2,1,0:T(8,128)(2,1)} %bitcast.36), calls=%async_computation.1 | async-start | bytes 2359296 | tf_op jit(solution)/shard_map/all_to_all | solution.py:479
  263.7 2.3 collective-permute-start.34
  263.8 3.0 collective-permute-start.35
  264.3 26.7 %collective-permute-start.36 = (bf16[8,64,768]{2,1,0:T(8,128)(2,1)}, bf16[8,64,768]{2,1,0:T(8,128)(2,1)}, u32[]{:S(2)}, u32[]{:S(2)}) collective-permute-start(bf16[8,64,768]{2,1,0:T(8,128)(2,1)} %get-tuple-element.222), channel_id=1, source_target_pairs={{0,3},{1,2},{2,1},{3,0},{4,7},{5,6},{6,5},{7,4},{8,11},{9,10},{10,... | collective-permute-start | bytes 2359304 | tf_op jit(solution)/shard_map/ppermute | solution.py:25
  265.3 31.4 %collective-permute-start.46 = (bf16[4,2,96,768]{3,2,1,0:T(8,128)(2,1)}, bf16[4,2,96,768]{3,2,1,0:T(8,128)(2,1)}, u32[]{:S(2)}, u32[]{:S(2)}) collective-permute-start(bf16[4,2,96,768]{3,2,1,0:T(8,128)(2,1)} %get-tuple-element.243), channel_id=1, source_target_pairs={{0,1},{1,0},{2,3},{3,2},{4,5},{5,4},{6,7},{7,6},{8,9},{9,8},{10,11... | collective-permute-start | bytes 3538952 | tf_op jit(solution)/shard_map/ppermute | solution.py:25
  268.4 28.3 %collective-permute-start.47 = (bf16[4,2,96,768]{3,2,1,0:T(8,128)(2,1)S(1)}, bf16[4,2,96,768]{3,2,1,0:T(8,128)(2,1)}, u32[]{:S(2)}, u32[]{:S(2)}) collective-permute-start(bf16[4,2,96,768]{3,2,1,0:T(8,128)(2,1)S(1)} %fusion.1), channel_id=1, source_target_pairs={{0,4},{4,0},{8,12},{12,8},{16,20},{20,16},{24,28},{28,24},{1,5},{5... | collective-permute-start | bytes 3538952 | tf_op jit(solution)/shard_map/ppermute | solution.py:25
  291.0 2.3 collective-permute-start.37
  291.1 3.0 collective-permute-start.38
  295.8 34.8 %collective-permute-start.44 = (bf16[4,2,96,768]{3,2,1,0:T(8,128)(2,1)S(1)}, bf16[4,2,96,768]{3,2,1,0:T(8,128)(2,1)}, u32[]{:S(2)}, u32[]{:S(2)}) collective-permute-start(bf16[4,2,96,768]{3,2,1,0:T(8,128)(2,1)S(1)} %fusion), channel_id=1, source_target_pairs={{0,4},{4,0},{8,12},{12,8},{16,20},{20,16},{24,28},{28,24},{1,5},{5... | collective-permute-start | bytes 3538952 | tf_op jit(solution)/shard_map/ppermute | solution.py:25
  299.8 35.4 %all-to-all-start.4 = ((bf16[4,192,768]{2,1,0:T(8,128)(2,1)}), bf16[4,192,768]{2,1,0:T(8,128)(2,1)S(1)}, u32[]{:S(2)}, u32[]{:S(2)}) async-start(bf16[4,192,768]{2,1,0:T(8,128)(2,1)} %bitcast.42), calls=%async_computation.4 | async-start | bytes 2359296 | tf_op jit(solution)/shard_map/all_to_all | solution.py:479
  305.2 26.2 %collective-permute-start.41 = (bf16[4,2,96,768]{3,2,1,0:T(8,128)(2,1)}, bf16[4,2,96,768]{3,2,1,0:T(8,128)(2,1)S(1)}, u32[]{:S(2)}, u32[]{:S(2)}) collective-permute-start(bf16[4,2,96,768]{3,2,1,0:T(8,128)(2,1)} %get-tuple-element.231), channel_id=1, source_target_pairs={{0,1},{1,0},{2,3},{3,2},{4,5},{5,4},{6,7},{7,6},{8,9},{9,8},{10,11... | collective-permute-start | bytes 3538952 | tf_op jit(solution)/shard_map/ppermute | solution.py:25
  306.4 24.2 %collective-permute-start.39 = (bf16[384,768]{1,0:T(8,128)(2,1)S(1)}, bf16[384,768]{1,0:T(8,128)(2,1)}, u32[]{:S(2)}, u32[]{:S(2)}) collective-permute-start(bf16[384,768]{1,0:T(8,128)(2,1)S(1)} %pad_maximum_fusion.5), channel_id=1, source_target_pairs={{0,2},{1,3},{2,0},{3,1},{4,6},{5,7},{6,4},{7,5},{8,10},{9,11},{10,... | collective-permute-start | bytes 1769480 | tf_op jit(solution)/shard_map/ppermute | solution.py:25
  307.9 22.7 %collective-permute-start.40 = (bf16[8,32,768]{2,1,0:T(8,128)(2,1)S(1)}, bf16[8,32,768]{2,1,0:T(8,128)(2,1)S(1)}, u32[]{:S(2)}, u32[]{:S(2)}) collective-permute-start(bf16[8,32,768]{2,1,0:T(8,128)(2,1)S(1)} %copy-done.5), channel_id=1, source_target_pairs={{0,2},{1,3},{2,0},{3,1},{4,6},{5,7},{6,4},{7,5},{8,10},{9,11},{10,... | collective-permute-start | bytes 1179656 | tf_op jit(solution)/shard_map/ppermute | solution.py:25
  308.5 1.2 collective-permute-start.42
  309.7 20.9 %collective-permute-start.43 = (bf16[16,768]{1,0:T(8,128)(2,1)S(1)}, bf16[16,768]{1,0:T(8,128)(2,1)S(1)}, u32[]{:S(2)}, u32[]{:S(2)}) collective-permute-start(bf16[16,768]{1,0:T(8,128)(2,1)S(1)} %add_convert_fusion.5), channel_id=1, source_target_pairs={{0,4},{4,0},{8,12},{12,8},{16,20},{20,16},{24,28},{28,24},{1,5},{5... | collective-permute-start | bytes 73736 | tf_op jit(solution)/shard_map/ppermute | solution.py:25
  334.7 12.5 %collective-permute-start.50 = (bf16[384,768]{1,0:T(8,128)(2,1)S(1)}, bf16[384,768]{1,0:T(8,128)(2,1)}, u32[]{:S(2)}, u32[]{:S(2)}) collective-permute-start(bf16[384,768]{1,0:T(8,128)(2,1)S(1)} %pad_maximum_fusion.5), channel_id=1, source_target_pairs={{0,1},{1,0},{2,3},{3,2},{4,5},{5,4},{6,7},{7,6},{8,9},{9,8},{10,11... | collective-permute-start | bytes 1769480 | tf_op jit(solution)/shard_map/ppermute | solution.py:25
  334.7 12.5 %collective-permute-start.51 = (bf16[384,768]{1,0:T(8,128)(2,1)}, bf16[384,768]{1,0:T(8,128)(2,1)}, u32[]{:S(2)}, u32[]{:S(2)}) collective-permute-start(bf16[384,768]{1,0:T(8,128)(2,1)} %collective-permute-done.39), channel_id=1, source_target_pairs={{0,1},{1,0},{2,3},{3,2},{4,5},{5,4},{6,7},{7,6},{8,9},{9,8},{10,11... | collective-permute-start | bytes 1769480 | tf_op jit(solution)/shard_map/ppermute | solution.py:25
  335.2 35.9 %all-to-all-start.3 = ((bf16[4,208,768]{2,1,0:T(8,128)(2,1)}), bf16[4,208,768]{2,1,0:T(8,128)(2,1)S(1)}, u32[]{:S(2)}, u32[]{:S(2)}) async-start(bf16[4,208,768]{2,1,0:T(8,128)(2,1)} %pad_maximum_fusion.1), calls=%async_computation.3 | async-start | bytes 2555904 | tf_op jit(solution)/shard_map/all_to_all | solution.py:479
  340.3 14.6 %collective-permute-start.49 = (bf16[8,32,768]{2,1,0:T(8,128)(2,1)}, bf16[8,32,768]{2,1,0:T(8,128)(2,1)}, u32[]{:S(2)}, u32[]{:S(2)}) collective-permute-start(bf16[8,32,768]{2,1,0:T(8,128)(2,1)} %get-tuple-element.253.refs_4_), channel_id=1, source_target_pairs={{0,2},{1,3},{2,0},{3,1},{4,6},{5,7},{6,4},{7,5},{8,10},{9,11},{10,... | collective-permute-start | bytes 1179656 | tf_op jit(solution)/shard_map/ppermute | solution.py:25
  343.6 11.2 %collective-permute-start.45 = (bf16[2,8,32,768]{3,2,1,0:T(8,128)(2,1)}, bf16[2,8,32,768]{3,2,1,0:T(8,128)(2,1)}, u32[]{:S(2)}, u32[]{:S(2)}) collective-permute-start(bf16[2,8,32,768]{3,2,1,0:T(8,128)(2,1)} %pad_maximum_fusion.8), channel_id=1, source_target_pairs={{0,1},{1,0},{2,3},{3,2},{4,5},{5,4},{6,7},{7,6},{8,9},{9,8},{10,11... | collective-permute-start | bytes 2359304 | tf_op jit(solution)/shard_map/ppermute | solution.py:25
  352.0 9.5 %collective-permute-start.48 = (bf16[192,768]{1,0:T(8,128)(2,1)S(1)}, bf16[192,768]{1,0:T(8,128)(2,1)S(1)}, u32[]{:S(2)}, u32[]{:S(2)}) collective-permute-start(bf16[192,768]{1,0:T(8,128)(2,1)S(1)} %reduce_sum.44), channel_id=1, source_target_pairs={{0,2},{1,3},{2,0},{3,1},{4,6},{5,7},{6,4},{7,5},{8,10},{9,11},{10,... | collective-permute-start | bytes 884744 | tf_op jit(solution)/shard_map/ppermute | solution.py:25
  371.4 3.2 collective-permute-start.56
  371.5 3.1 collective-permute-start.57
  373.1 4.4 %collective-permute-start.52 = (bf16[2,8,32,768]{3,2,1,0:T(8,128)(2,1)S(1)}, bf16[2,8,32,768]{3,2,1,0:T(8,128)(2,1)S(1)}, u32[]{:S(2)}, u32[]{:S(2)}) collective-permute-start(bf16[2,8,32,768]{3,2,1,0:T(8,128)(2,1)S(1)} %pad_maximum_fusion.9), channel_id=1, source_target_pairs={{0,1},{1,0},{2,3},{3,2},{4,5},{5,4},{6,7},{7,6},{8,9},{9,8},{10,11... | collective-permute-start | bytes 2359304 | tf_op jit(solution)/shard_map/ppermute | solution.py:25
  373.2 9.9 %collective-permute-start.53 = (bf16[208,768]{1,0:T(8,128)(2,1)S(1)}, bf16[208,768]{1,0:T(8,128)(2,1)S(1)}, u32[]{:S(2)}, u32[]{:S(2)}) collective-permute-start(bf16[208,768]{1,0:T(8,128)(2,1)S(1)} %reduce_sum.45), channel_id=1, source_target_pairs={{0,2},{1,3},{2,0},{3,1},{4,6},{5,7},{6,4},{7,5},{8,10},{9,11},{10,... | collective-permute-start | bytes 958472 | tf_op jit(solution)/shard_map/ppermute | solution.py:25
  383.1 2.1 collective-permute-start.54
  383.2 2.0 collective-permute-start.55
  (39 other events, 243.9 us)
